TPU v7x, 512 devices: a whole 4x4x16 slice. The times are simulated.
512 devices in a mesh: grain: 16 (over x, y_hi, core), space: 32 (over z, y_lo).
Axes of the slice: x: 4, y: 4 (y_hi: 2, y_lo: 2; y = y_hi * 2 + y_lo), z: 16, core: 2. Of those that a mesh axis runs over, the one named last changes fastest.
Arguments:
- labels: int32 [32, 256, 256], P(None, 'space'), may hold values from 0 to 63, as said below
- density: float32 [32, 256, 256], P('grain', 'space'), may hold values from 0.05 to 0.95
Outputs:
- grain_fields: float32 [64, 32, 256, 256], P('grain', None, 'space')
- density_field: float32 [32, 256, 256], P('grain', 'space')
Inputs may be any that keep to these rules, and one draw needn't show every extreme that they name: Within each aligned block of 2 x 2 x 8 cells (thickness, first and second in-plane dimension) the labels take at most three values.
All inputs are finite; a program needn't handle non-finite values.
Results may differ from a plain program's by a relative error of at most 0.0001.
Values sent between devices are 32-bit elements; how exact they have to be, the bound alone decides.
No kernel may reach another device: no remote copies, remote signals or barrier semaphores. Data moves between devices by JAX's collectives and lax.ppermute only.
A program may use at most 64 MiB of HBM per device.

v0:
```python
import jax
import jax.numpy as jnp
from jax import lax
from jax.sharding import PartitionSpec as P

GDEV = 4
STEPS = 2
NSUB = 4


bulk_coef = 8.0
grain_coef = 1.0
grad_density = 1.0
grad_grain = 1.0
mobility = 1.0
relax_rate = 2.0
grain_step = 0.008
density_step = 0.004


def extended(block, sides, width):
    for axis, dim in sides:
        count = lax.axis_size(axis)
        forward = [(i, i + 1) for i in range(count - 1)]
        forward.append((count - 1, 0))
        backward = [(target, source) for source, target in forward]
        low = lax.ppermute(
            lax.slice_in_dim(block, block.shape[dim] - width, None, axis=dim), axis, forward
        )
        high = lax.ppermute(lax.slice_in_dim(block, 0, width, axis=dim), axis, backward)
        block = jnp.concatenate([low, block, high], axis=dim)
    return block


def grain_rate(order, dens, square):
    return grain_coef * (
        12.0 * (1.0 - dens) * order - 12.0 * (2.0 - dens) * order * order + 12.0 * order * square
    )


def bulk_potential(dens, square, cube):
    return bulk_coef * (
        2.0 * dens * (1.0 - dens) * (1.0 - dens) - 2.0 * dens * dens * (1.0 - dens)
    ) + grain_coef * (2.0 * dens - 6.0 * square + 4.0 * cube)


def order_laplace(padded):
    inner = padded[:, :, 1:-1]
    zsum = jnp.roll(inner, 1, 1) + jnp.roll(inner, -1, 1)
    xsum = padded[:, :, 2:] + padded[:, :, :-2]
    ysum = jnp.roll(inner, 1, 3) + jnp.roll(inner, -1, 3)
    return zsum + xsum + ysum - 6.0 * inner


def tile_laplace(padded):
    inner = padded[1:-1, 1:-1]
    zsum = padded[2:, 1:-1] + padded[:-2, 1:-1]
    xsum = padded[1:-1, 2:] + padded[1:-1, :-2]
    ysum = jnp.roll(inner, 1, 2) + jnp.roll(inner, -1, 2)
    return zsum + xsum + ysum - 6.0 * inner


def density_steps(dens, square_tile, cube_tile):
    for sub in range(NSUB):
        padded = extended(dens, (("grain", 0), ("space", 1)), 1)
        potential = bulk_potential(dens, square_tile, cube_tile) - grad_density * tile_laplace(
            padded
        )
        padded_pot = extended(potential, (("grain", 0), ("space", 1)), 1)
        dens = dens + density_step * mobility * tile_laplace(padded_pot)
    return dens


def per_device(labels, density):
    tile_rows = density.shape[0]
    grain_index = lax.axis_index("grain")
    grain_ids = grain_index * GDEV + jnp.arange(GDEV, dtype=jnp.int32)
    dens = density
    full_density = lax.all_gather(dens, "grain", axis=0, tiled=True)
    orders = jnp.where(
        labels[None] == grain_ids[:, None, None, None],
        full_density[None],
        jnp.zeros_like(full_density)[None],
    )
    square = full_density * full_density
    square_tile = dens
    for step in range(STEPS):
        if step > 0:
            full_density = lax.all_gather(dens, "grain", axis=0, tiled=True)
        padded = extended(orders, (("space", 2),), 1)
        laplace_orders = order_laplace(padded)
        orders = orders - grain_step * relax_rate * (
            grain_rate(orders, full_density[None], square[None]) - grad_grain * laplace_orders
        )
        local_square = jnp.sum(orders * orders, axis=0)
        local_cube = jnp.sum(orders * orders * orders, axis=0)
        square, cube_full = lax.psum((local_square, local_cube), "grain")
        start = grain_index * tile_rows
        square_tile = lax.dynamic_slice_in_dim(square, start, tile_rows, 0)
        cube_tile = lax.dynamic_slice_in_dim(cube_full, start, tile_rows, 0)
        dens = density_steps(dens, square_tile, cube_tile)
    return (orders, dens)


def solution(mesh):
    return jax.shard_map(
        per_device,
        mesh=mesh,
        in_specs=(P(None, "space", None), P("grain", "space", None)),
        out_specs=(P("grain", None, "space", None), P("grain", "space", None)),
        check_vma=False,
    )
```

profile of v0, /device:TPU:1, one launch (start us, length us, event | category | flops | bytes accessed | tf_op | source)
XLA Modules:
  0.0 727.6 jit_solution(11613534310505636885)
XLA Ops:
  7.2 26.7 %all_gather.6 = f32[32,8,256]{2,1,0:T(8,128)S(1)} all-gather(f32[2,8,256]{2,1,0:T(8,128)} %param.3), channel_id=1, replica_groups=mesh['grain'=16,'space'=32] {'grain'}, dimensions={0}, use_global_device_ids=true | all-gather | bytes 278528 | tf_op jit(solution)/shard_map/all_gather | solution.py:79
  35.8 11.2 %collective-permute-start = (f32[4,32,1,256]{3,1,2,0:T(8,128)S(1)}, f32[4,32,1,256]{3,1,2,0:T(8,128)S(1)}, u32[]{:S(2)}, u32[]{:S(2)}) collective-permute-start(f32[4,32,1,256]{3,1,2,0:T(8,128)S(1)} %get-tuple-element.30), channel_id=1, source_target_pairs={{1,0},{2,1},{3,2},{4,3},{5,4},{6,5},{7,6},{8,7},{9,8},{10,9},{11,1... | collective-permute-start | bytes 393224 | tf_op jit(solution)/shard_map/ppermute | solution.py:30
  51.3 4.7 collective-permute-start.3
  61.5 5.5 collective-permute-start.4
  70.3 4.5 fusion
  77.2 5.5 collective-permute-start.34
  86.4 146.4 %all-reduce.7.cloned.1.call-done = (f32[32,8,256]{2,0,1:T(8,128)}, f32[32,8,256]{2,0,1:T(8,128)}) async-done(((f32[32,8,256]{2,0,1:T(8,128)}, f32[32,8,256]{2,0,1:T(8,128)}), (f32[32,8,256]{2,0,1:T(8,128)}, f32[32,8,256]{2,0,1:T(8,128)})) %all-reduce.7.cloned.1.call-update) | async-done | bytes 524304 | tf_op jit(solution)/shard_map/psum | solution.py:97
  235.6 3.2 collective-permute-start.6
  238.8 3.9 collective-permute-start.7
  242.7 3.3 collective-permute-done.7
  246.0 5.7 collective-permute-start.8
  253.7 4.5 collective-permute-done.9
  258.3 9.5 %collective-permute-start.10 = (f32[1,8,256]{2,0,1:T(1,128)S(1)}, f32[1,8,256]{2,0,1:T(1,128)S(1)}, u32[]{:S(2)}, u32[]{:S(2)}) collective-permute-start(f32[1,8,256]{2,0,1:T(1,128)S(1)} %get-tuple-element.157), channel_id=1, source_target_pairs={{32,0},{64,32},{96,64},{128,96},{160,128},{192,160},{224,192},{256... | collective-permute-start | bytes 24584 | tf_op jit(solution)/shard_map/ppermute | solution.py:30
  272.8 3.4 collective-permute-start.13
  276.2 3.0 collective-permute-done.13
  280.3 8.6 %collective-permute-start.14 = (f32[1,8,256]{2,0,1:T(1,128)S(1)}, f32[1,8,256]{2,0,1:T(1,128)S(1)}, u32[]{:S(2)}, u32[]{:S(2)}) collective-permute-start(f32[1,8,256]{2,0,1:T(1,128)S(1)} %get-tuple-element.147), channel_id=1, source_target_pairs={{32,0},{64,32},{96,64},{128,96},{160,128},{192,160},{224,192},{256... | collective-permute-start | bytes 24584 | tf_op jit(solution)/shard_map/ppermute | solution.py:30
  293.9 3.4 collective-permute-start.17
  297.3 3.0 collective-permute-done.17
  300.4 8.6 %collective-permute-start.18 = (f32[1,8,256]{2,0,1:T(1,128)S(1)}, f32[1,8,256]{2,0,1:T(1,128)S(1)}, u32[]{:S(2)}, u32[]{:S(2)}) collective-permute-start(f32[1,8,256]{2,0,1:T(1,128)S(1)} %get-tuple-element.145), channel_id=1, source_target_pairs={{32,0},{64,32},{96,64},{128,96},{160,128},{192,160},{224,192},{256... | collective-permute-start | bytes 24584 | tf_op jit(solution)/shard_map/ppermute | solution.py:30
  314.1 3.4 collective-permute-start.21
  321.6 8.7 %collective-permute-start.22 = (f32[1,8,256]{2,0,1:T(1,128)S(1)}, f32[1,8,256]{2,0,1:T(1,128)S(1)}, u32[]{:S(2)}, u32[]{:S(2)}) collective-permute-start(f32[1,8,256]{2,0,1:T(1,128)S(1)} %get-tuple-element.135), channel_id=1, source_target_pairs={{32,0},{64,32},{96,64},{128,96},{160,128},{192,160},{224,192},{256... | collective-permute-start | bytes 24584 | tf_op jit(solution)/shard_map/ppermute | solution.py:30
  335.3 3.4 collective-permute-start.25
  341.9 8.6 %collective-permute-start.26 = (f32[1,8,256]{2,0,1:T(1,128)S(1)}, f32[1,8,256]{2,0,1:T(1,128)S(1)}, u32[]{:S(2)}, u32[]{:S(2)}) collective-permute-start(f32[1,8,256]{2,0,1:T(1,128)S(1)} %get-tuple-element.133), channel_id=1, source_target_pairs={{32,0},{64,32},{96,64},{128,96},{160,128},{192,160},{224,192},{256... | collective-permute-start | bytes 24584 | tf_op jit(solution)/shard_map/ppermute | solution.py:30
  355.5 3.4 collective-permute-start.29
  363.0 8.6 %collective-permute-start.30 = (f32[1,8,256]{2,0,1:T(1,128)S(1)}, f32[1,8,256]{2,0,1:T(1,128)S(1)}, u32[]{:S(2)}, u32[]{:S(2)}) collective-permute-start(f32[1,8,256]{2,0,1:T(1,128)S(1)} %get-tuple-element.123), channel_id=1, source_target_pairs={{32,0},{64,32},{96,64},{128,96},{160,128},{192,160},{224,192},{256... | collective-permute-start | bytes 24584 | tf_op jit(solution)/shard_map/ppermute | solution.py:30
  376.6 3.4 collective-permute-start.33
  383.2 26.2 %all_gather.7 = f32[32,8,256]{2,1,0:T(8,128)S(1)} all-gather(f32[2,8,256]{2,1,0:T(8,128)S(1)} %copy.33), channel_id=1, replica_groups=mesh['grain'=16,'space'=32] {'grain'}, dimensions={0}, use_global_device_ids=true | all-gather | bytes 278528 | tf_op jit(solution)/shard_map/all_gather | solution.py:89
  411.4 5.0 collective-permute-start.37
  417.3 3.0 fusion.1
  422.4 3.4 collective-permute-start.39
  428.8 143.0 %all-reduce.5.cloned.1.call-done = (f32[32,8,256]{2,0,1:T(8,128)}, f32[32,8,256]{2,0,1:T(8,128)}) async-done(((f32[32,8,256]{2,0,1:T(8,128)}, f32[32,8,256]{2,0,1:T(8,128)}), (f32[32,8,256]{2,0,1:T(8,128)}, f32[32,8,256]{2,0,1:T(8,128)})) %all-reduce.5.cloned.1.call-update) | async-done | bytes 524304 | tf_op jit(solution)/shard_map/psum | solution.py:97
  572.9 3.2 collective-permute-start.40
  576.1 3.9 collective-permute-start.41
  580.1 3.3 collective-permute-done.41
  583.4 5.7 collective-permute-start.42
  591.0 4.5 collective-permute-done.43
  595.6 9.4 %collective-permute-start.44 = (f32[1,8,256]{2,0,1:T(1,128)S(1)}, f32[1,8,256]{2,0,1:T(1,128)S(1)}, u32[]{:S(2)}, u32[]{:S(2)}) collective-permute-start(f32[1,8,256]{2,0,1:T(1,128)S(1)} %get-tuple-element.109), channel_id=1, source_target_pairs={{32,0},{64,32},{96,64},{128,96},{160,128},{192,160},{224,192},{256... | collective-permute-start | bytes 24584 | tf_op jit(solution)/shard_map/ppermute | solution.py:30
  610.0 3.4 collective-permute-start.47
  617.5 8.6 %collective-permute-start.48 = (f32[1,8,256]{2,0,1:T(1,128)S(1)}, f32[1,8,256]{2,0,1:T(1,128)S(1)}, u32[]{:S(2)}, u32[]{:S(2)}) collective-permute-start(f32[1,8,256]{2,0,1:T(1,128)S(1)} %get-tuple-element.99), channel_id=1, source_target_pairs={{32,0},{64,32},{96,64},{128,96},{160,128},{192,160},{224,192},{256... | collective-permute-start | bytes 24584 | tf_op jit(solution)/shard_map/ppermute | solution.py:30
  631.1 3.4 collective-permute-start.51
  637.7 8.6 %collective-permute-start.52 = (f32[1,8,256]{2,0,1:T(1,128)S(1)}, f32[1,8,256]{2,0,1:T(1,128)S(1)}, u32[]{:S(2)}, u32[]{:S(2)}) collective-permute-start(f32[1,8,256]{2,0,1:T(1,128)S(1)} %get-tuple-element.97), channel_id=1, source_target_pairs={{32,0},{64,32},{96,64},{128,96},{160,128},{192,160},{224,192},{256... | collective-permute-start | bytes 24584 | tf_op jit(solution)/shard_map/ppermute | solution.py:30
  651.3 3.4 collective-permute-start.55
  658.8 8.6 %collective-permute-start.56 = (f32[1,8,256]{2,0,1:T(1,128)S(1)}, f32[1,8,256]{2,0,1:T(1,128)S(1)}, u32[]{:S(2)}, u32[]{:S(2)}) collective-permute-start(f32[1,8,256]{2,0,1:T(1,128)S(1)} %get-tuple-element.87), channel_id=1, source_target_pairs={{32,0},{64,32},{96,64},{128,96},{160,128},{192,160},{224,192},{256... | collective-permute-start | bytes 24584 | tf_op jit(solution)/shard_map/ppermute | solution.py:30
  672.4 3.4 collective-permute-start.59
  678.9 8.6 %collective-permute-start.60 = (f32[1,8,256]{2,0,1:T(1,128)S(1)}, f32[1,8,256]{2,0,1:T(1,128)S(1)}, u32[]{:S(2)}, u32[]{:S(2)}) collective-permute-start(f32[1,8,256]{2,0,1:T(1,128)S(1)} %get-tuple-element.85), channel_id=1, source_target_pairs={{32,0},{64,32},{96,64},{128,96},{160,128},{192,160},{224,192},{256... | collective-permute-start | bytes 24584 | tf_op jit(solution)/shard_map/ppermute | solution.py:30
  692.5 3.4 collective-permute-start.63
  700.0 8.6 %collective-permute-start.64 = (f32[1,8,256]{2,0,1:T(1,128)S(1)}, f32[1,8,256]{2,0,1:T(1,128)S(1)}, u32[]{:S(2)}, u32[]{:S(2)}) collective-permute-start(f32[1,8,256]{2,0,1:T(1,128)S(1)} %get-tuple-element.75), channel_id=1, source_target_pairs={{32,0},{64,32},{96,64},{128,96},{160,128},{192,160},{224,192},{256... | collective-permute-start | bytes 24584 | tf_op jit(solution)/shard_map/ppermute | solution.py:30
  713.6 3.4 collective-permute-start.67
  (228 shorter events, 135.4 us)
Async XLA Ops:
  7.2 225.6 %all-reduce.7.cloned.1.call-start = ((), (), s32[]{:S(2)}) async-start(), calls=%async_computation.1 | async-start | bytes 1048576 | tf_op jit(solution)/shard_map/psum | solution.py:97
  35.8 33.2 %collective-permute-start = (f32[4,32,1,256]{3,1,2,0:T(8,128)S(1)}, f32[4,32,1,256]{3,1,2,0:T(8,128)S(1)}, u32[]{:S(2)}, u32[]{:S(2)}) collective-permute-start(f32[4,32,1,256]{3,1,2,0:T(8,128)S(1)} %get-tuple-element.30), channel_id=1, source_target_pairs={{1,0},{2,1},{3,2},{4,3},{5,4},{6,5},{7,6},{8,7},{9,8},{10,9},{11,1... | collective-permute-start | bytes 393224 | tf_op jit(solution)/shard_map/ppermute | solution.py:30
  46.9 22.0 %collective-permute-start.1 = (f32[4,32,1,256]{3,1,2,0:T(8,128)S(1)}, f32[4,32,1,256]{3,1,2,0:T(8,128)S(1)}, u32[]{:S(2)}, u32[]{:S(2)}) collective-permute-start(f32[4,32,1,256]{3,1,2,0:T(8,128)S(1)} %get-tuple-element.31), channel_id=1, source_target_pairs={{0,1},{1,2},{2,3},{3,4},{4,5},{5,6},{6,7},{7,8},{8,9},{9,10},{10,1... | collective-permute-start | bytes 393224 | tf_op jit(solution)/shard_map/ppermute | solution.py:27
  48.9 12.0 %collective-permute-start.2 = (f32[1,8,256]{2,0,1:T(1,128)S(1)}, f32[1,8,256]{2,0,1:T(1,128)S(1)}, u32[]{:S(2)}, u32[]{:S(2)}) collective-permute-start(f32[1,8,256]{2,0,1:T(1,128)S(1)} %copy.22), channel_id=1, source_target_pairs={{32,0},{64,32},{96,64},{128,96},{160,128},{192,160},{224,192},{256... | collective-permute-start | bytes 24584 | tf_op jit(solution)/shard_map/ppermute | solution.py:30
  51.3 9.6 %collective-permute-start.3 = (f32[1,8,256]{2,0,1:T(1,128)S(1)}, f32[1,8,256]{2,0,1:T(1,128)S(1)}, u32[]{:S(2)}, u32[]{:S(2)}) collective-permute-start(f32[1,8,256]{2,0,1:T(1,128)S(1)} %copy.24), channel_id=1, source_target_pairs={{0,32},{32,64},{64,96},{96,128},{128,160},{160,192},{192,224},{224... | collective-permute-start | bytes 24584 | tf_op jit(solution)/shard_map/ppermute | solution.py:27
  61.5 172.3 %collective-permute-start.4 = (f32[4,1,256]{2,0,1:T(4,128)}, f32[4,1,256]{2,0,1:T(4,128)}, u32[]{:S(2)}, u32[]{:S(2)}) collective-permute-start(f32[4,1,256]{2,0,1:T(4,128)} %get-tuple-element.72), channel_id=1, source_target_pairs={{1,0},{2,1},{3,2},{4,3},{5,4},{6,5},{7,6},{8,7},{9,8},{10,9},{11,1... | collective-permute-start | bytes 12296 | tf_op jit(solution)/shard_map/ppermute | solution.py:30
  67.0 166.9 %collective-permute-start.5 = (f32[4,1,256]{2,0,1:T(4,128)}, f32[4,1,256]{2,0,1:T(4,128)}, u32[]{:S(2)}, u32[]{:S(2)}) collective-permute-start(f32[4,1,256]{2,0,1:T(4,128)} %get-tuple-element.73), channel_id=1, source_target_pairs={{0,1},{1,2},{2,3},{3,4},{4,5},{5,6},{6,7},{7,8},{8,9},{9,10},{10,1... | collective-permute-start | bytes 12296 | tf_op jit(solution)/shard_map/ppermute | solution.py:27
  77.2 339.4 %collective-permute-start.34 = (f32[4,32,1,256]{3,1,2,0:T(8,128)S(1)}, f32[4,32,1,256]{3,1,2,0:T(8,128)S(1)}, u32[]{:S(2)}, u32[]{:S(2)}) collective-permute-start(f32[4,32,1,256]{3,1,2,0:T(8,128)S(1)} %get-tuple-element.20), channel_id=1, source_target_pairs={{1,0},{2,1},{3,2},{4,3},{5,4},{6,5},{7,6},{8,7},{9,8},{10,9},{11,1... | collective-permute-start | bytes 393224 | tf_op jit(solution)/shard_map/ppermute | solution.py:30
  82.7 333.9 %collective-permute-start.35 = (f32[4,32,1,256]{3,1,2,0:T(8,128)S(1)}, f32[4,32,1,256]{3,1,2,0:T(8,128)S(1)}, u32[]{:S(2)}, u32[]{:S(2)}) collective-permute-start(f32[4,32,1,256]{3,1,2,0:T(8,128)S(1)} %get-tuple-element.21), channel_id=1, source_target_pairs={{0,1},{1,2},{2,3},{3,4},{4,5},{5,6},{6,7},{7,8},{8,9},{9,10},{10,1... | collective-permute-start | bytes 393224 | tf_op jit(solution)/shard_map/ppermute | solution.py:27
  84.6 487.3 %all-reduce.5.cloned.1.call-start = ((), (), s32[]{:S(2)}) async-start(), calls=%async_computation | async-start | bytes 1048576 | tf_op jit(solution)/shard_map/psum | solution.py:97
  235.6 7.2 collective-permute-start.6
  238.8 7.2 collective-permute-start.7
  246.0 7.7 %collective-permute-start.8 = (f32[4,1,256]{2,0,1:T(4,128)S(1)}, f32[4,1,256]{2,0,1:T(4,128)S(1)}, u32[]{:S(2)}, u32[]{:S(2)}) collective-permute-start(f32[4,1,256]{2,0,1:T(4,128)S(1)} %get-tuple-element.70), channel_id=1, source_target_pairs={{1,0},{2,1},{3,2},{4,3},{5,4},{6,5},{7,6},{8,7},{9,8},{10,9},{11,1... | collective-permute-start | bytes 12296 | tf_op jit(solution)/shard_map/ppermute | solution.py:30
  251.7 6.5 collective-permute-start.9
  258.3 11.5 %collective-permute-start.10 = (f32[1,8,256]{2,0,1:T(1,128)S(1)}, f32[1,8,256]{2,0,1:T(1,128)S(1)}, u32[]{:S(2)}, u32[]{:S(2)}) collective-permute-start(f32[1,8,256]{2,0,1:T(1,128)S(1)} %get-tuple-element.157), channel_id=1, source_target_pairs={{32,0},{64,32},{96,64},{128,96},{160,128},{192,160},{224,192},{256... | collective-permute-start | bytes 24584 | tf_op jit(solution)/shard_map/ppermute | solution.py:30
  270.8 5.4 collective-permute-start.12
  272.8 6.5 collective-permute-start.13
  280.3 10.6 %collective-permute-start.14 = (f32[1,8,256]{2,0,1:T(1,128)S(1)}, f32[1,8,256]{2,0,1:T(1,128)S(1)}, u32[]{:S(2)}, u32[]{:S(2)}) collective-permute-start(f32[1,8,256]{2,0,1:T(1,128)S(1)} %get-tuple-element.147), channel_id=1, source_target_pairs={{32,0},{64,32},{96,64},{128,96},{160,128},{192,160},{224,192},{256... | collective-permute-start | bytes 24584 | tf_op jit(solution)/shard_map/ppermute | solution.py:30
  291.9 5.4 collective-permute-start.16
  293.9 6.5 collective-permute-start.17
  300.4 10.6 %collective-permute-start.18 = (f32[1,8,256]{2,0,1:T(1,128)S(1)}, f32[1,8,256]{2,0,1:T(1,128)S(1)}, u32[]{:S(2)}, u32[]{:S(2)}) collective-permute-start(f32[1,8,256]{2,0,1:T(1,128)S(1)} %get-tuple-element.145), channel_id=1, source_target_pairs={{32,0},{64,32},{96,64},{128,96},{160,128},{192,160},{224,192},{256... | collective-permute-start | bytes 24584 | tf_op jit(solution)/shard_map/ppermute | solution.py:30
  314.1 6.5 collective-permute-start.21
  321.6 10.7 %collective-permute-start.22 = (f32[1,8,256]{2,0,1:T(1,128)S(1)}, f32[1,8,256]{2,0,1:T(1,128)S(1)}, u32[]{:S(2)}, u32[]{:S(2)}) collective-permute-start(f32[1,8,256]{2,0,1:T(1,128)S(1)} %get-tuple-element.135), channel_id=1, source_target_pairs={{32,0},{64,32},{96,64},{128,96},{160,128},{192,160},{224,192},{256... | collective-permute-start | bytes 24584 | tf_op jit(solution)/shard_map/ppermute | solution.py:30
  335.3 6.5 collective-permute-start.25
  341.9 10.6 %collective-permute-start.26 = (f32[1,8,256]{2,0,1:T(1,128)S(1)}, f32[1,8,256]{2,0,1:T(1,128)S(1)}, u32[]{:S(2)}, u32[]{:S(2)}) collective-permute-start(f32[1,8,256]{2,0,1:T(1,128)S(1)} %get-tuple-element.133), channel_id=1, source_target_pairs={{32,0},{64,32},{96,64},{128,96},{160,128},{192,160},{224,192},{256... | collective-permute-start | bytes 24584 | tf_op jit(solution)/shard_map/ppermute | solution.py:30
  355.5 6.5 collective-permute-start.29
  363.0 10.6 %collective-permute-start.30 = (f32[1,8,256]{2,0,1:T(1,128)S(1)}, f32[1,8,256]{2,0,1:T(1,128)S(1)}, u32[]{:S(2)}, u32[]{:S(2)}) collective-permute-start(f32[1,8,256]{2,0,1:T(1,128)S(1)} %get-tuple-element.123), channel_id=1, source_target_pairs={{32,0},{64,32},{96,64},{128,96},{160,128},{192,160},{224,192},{256... | collective-permute-start | bytes 24584 | tf_op jit(solution)/shard_map/ppermute | solution.py:30
  376.6 6.5 collective-permute-start.33
  409.4 11.1 %collective-permute-start.36 = (f32[1,8,256]{2,0,1:T(1,128)S(1)}, f32[1,8,256]{2,0,1:T(1,128)S(1)}, u32[]{:S(2)}, u32[]{:S(2)}) collective-permute-start(f32[1,8,256]{2,0,1:T(1,128)S(1)} %get-tuple-element.121), channel_id=1, source_target_pairs={{32,0},{64,32},{96,64},{128,96},{160,128},{192,160},{224,192},{256... | collective-permute-start | bytes 24584 | tf_op jit(solution)/shard_map/ppermute | solution.py:30
  411.4 9.0 %collective-permute-start.37 = (f32[1,8,256]{2,0,1:T(1,128)S(1)}, f32[1,8,256]{2,0,1:T(1,128)S(1)}, u32[]{:S(2)}, u32[]{:S(2)}) collective-permute-start(f32[1,8,256]{2,0,1:T(1,128)S(1)} %get-tuple-element.120), channel_id=1, source_target_pairs={{0,32},{32,64},{64,96},{96,128},{128,160},{160,192},{192,224},{224... | collective-permute-start | bytes 24584 | tf_op jit(solution)/shard_map/ppermute | solution.py:27
  420.5 7.0 collective-permute-start.38
  422.4 6.5 collective-permute-start.39
  572.9 7.2 collective-permute-start.40
  576.1 7.2 collective-permute-start.41
  583.4 7.7 %collective-permute-start.42 = (f32[4,1,256]{2,0,1:T(4,128)S(1)}, f32[4,1,256]{2,0,1:T(4,128)S(1)}, u32[]{:S(2)}, u32[]{:S(2)}) collective-permute-start(f32[4,1,256]{2,0,1:T(4,128)S(1)} %get-tuple-element.54), channel_id=1, source_target_pairs={{1,0},{2,1},{3,2},{4,3},{5,4},{6,5},{7,6},{8,7},{9,8},{10,9},{11,1... | collective-permute-start | bytes 12296 | tf_op jit(solution)/shard_map/ppermute | solution.py:30
  589.0 6.5 collective-permute-start.43
  595.6 11.4 %collective-permute-start.44 = (f32[1,8,256]{2,0,1:T(1,128)S(1)}, f32[1,8,256]{2,0,1:T(1,128)S(1)}, u32[]{:S(2)}, u32[]{:S(2)}) collective-permute-start(f32[1,8,256]{2,0,1:T(1,128)S(1)} %get-tuple-element.109), channel_id=1, source_target_pairs={{32,0},{64,32},{96,64},{128,96},{160,128},{192,160},{224,192},{256... | collective-permute-start | bytes 24584 | tf_op jit(solution)/shard_map/ppermute | solution.py:30
  610.0 6.5 collective-permute-start.47
  617.5 10.6 %collective-permute-start.48 = (f32[1,8,256]{2,0,1:T(1,128)S(1)}, f32[1,8,256]{2,0,1:T(1,128)S(1)}, u32[]{:S(2)}, u32[]{:S(2)}) collective-permute-start(f32[1,8,256]{2,0,1:T(1,128)S(1)} %get-tuple-element.99), channel_id=1, source_target_pairs={{32,0},{64,32},{96,64},{128,96},{160,128},{192,160},{224,192},{256... | collective-permute-start | bytes 24584 | tf_op jit(solution)/shard_map/ppermute | solution.py:30
  631.1 6.5 collective-permute-start.51
  637.7 10.6 %collective-permute-start.52 = (f32[1,8,256]{2,0,1:T(1,128)S(1)}, f32[1,8,256]{2,0,1:T(1,128)S(1)}, u32[]{:S(2)}, u32[]{:S(2)}) collective-permute-start(f32[1,8,256]{2,0,1:T(1,128)S(1)} %get-tuple-element.97), channel_id=1, source_target_pairs={{32,0},{64,32},{96,64},{128,96},{160,128},{192,160},{224,192},{256... | collective-permute-start | bytes 24584 | tf_op jit(solution)/shard_map/ppermute | solution.py:30
  651.3 6.5 collective-permute-start.55
  658.8 10.6 %collective-permute-start.56 = (f32[1,8,256]{2,0,1:T(1,128)S(1)}, f32[1,8,256]{2,0,1:T(1,128)S(1)}, u32[]{:S(2)}, u32[]{:S(2)}) collective-permute-start(f32[1,8,256]{2,0,1:T(1,128)S(1)} %get-tuple-element.87), channel_id=1, source_target_pairs={{32,0},{64,32},{96,64},{128,96},{160,128},{192,160},{224,192},{256... | collective-permute-start | bytes 24584 | tf_op jit(solution)/shard_map/ppermute | solution.py:30
  672.4 6.5 collective-permute-start.59
  678.9 10.6 %collective-permute-start.60 = (f32[1,8,256]{2,0,1:T(1,128)S(1)}, f32[1,8,256]{2,0,1:T(1,128)S(1)}, u32[]{:S(2)}, u32[]{:S(2)}) collective-permute-start(f32[1,8,256]{2,0,1:T(1,128)S(1)} %get-tuple-element.85), channel_id=1, source_target_pairs={{32,0},{64,32},{96,64},{128,96},{160,128},{192,160},{224,192},{256... | collective-permute-start | bytes 24584 | tf_op jit(solution)/shard_map/ppermute | solution.py:30
  692.5 6.5 collective-permute-start.63
  700.0 10.6 %collective-permute-start.64 = (f32[1,8,256]{2,0,1:T(1,128)S(1)}, f32[1,8,256]{2,0,1:T(1,128)S(1)}, u32[]{:S(2)}, u32[]{:S(2)}) collective-permute-start(f32[1,8,256]{2,0,1:T(1,128)S(1)} %get-tuple-element.75), channel_id=1, source_target_pairs={{32,0},{64,32},{96,64},{128,96},{160,128},{192,160},{224,192},{256... | collective-permute-start | bytes 24584 | tf_op jit(solution)/shard_map/ppermute | solution.py:30
  713.6 6.5 collective-permute-start.67
  (36 other events, 793.5 us)
Sparse Core Ops, SparseCore 0:
  84.7 148.0 all-reduce.6
  420.5 151.3 all-reduce.4
where the time goes:
time: 734 us; the launch traced here: 728 us
  waiting for transfers between devices  355 us (48%)
  starting transfers between devices  268 us (37%)
  blocking collectives  52.9 us (7%)
  other arithmetic  19.4 us (3%)
  local copies, waits for them, and re-layouts  17.1 us (2%)
  between operations  15.1 us (2%)
    psum x2, waiting for transfers between devices, per_device(): square, cube_full = lax.psum((local_square, local_cube), 'grain')  289 us
    ppermute x34, starting transfers between devices, extended(): lax.ppermute(lax.slice_in_dim(block, 0, width, axis=dim), axis, backward)  174 us
    ppermute x34, starting transfers between devices, extended(): lax.ppermute(lax.slice_in_dim(block, block.shape[dim] - width, None, axis...  93.8 us
    ppermute x34, waiting for transfers between devices, extended(): lax.ppermute(lax.slice_in_dim(block, block.shape[dim] - width, None, axis...  65.6 us
    all_gather x2, blocking collectives, per_device(): full_density = lax.all_gather(dens, 'grain', axis=0, tiled=True)  52.9 us
  transfers between devices with their start and end apart: 70, of which 31 were waited for; matrix products, arithmetic and copies ran while one was open for 4% of the time, Pallas kernels for 0%

commit v1 on v0

v1 whole, which is shorter than its diff:
```python
import functools

import jax
import jax.numpy as jnp
from jax import lax
from jax.experimental import pallas as pl
from jax.experimental.pallas import tpu as pltpu
from jax.sharding import PartitionSpec as P

GDEV = 4
NSUB = 4
LAYERS = 32
WIDTH = 256
ROWS = 56
MID = 24
TILE = 15
BASE = 6

rate = 0.008 * 2.0
density_step = 0.004

SHIFTS = (
    (0, 0),
    (1, 0),
    (-1, 0),
    (0, 1),
    (0, -1),
    (1, 1),
    (1, -1),
    (-1, 1),
    (-1, -1),
    (2, 0),
    (-2, 0),
    (0, 2),
    (0, -2),
)
SLOT = {pair: index for index, pair in enumerate(SHIFTS)}
INNER = ((0, 0, 0), (1, 0, 0), (-1, 0, 0), (0, 1, 0), (0, -1, 0), (0, 0, 1), (0, 0, -1))
OUTER = tuple(
    (dz, dx, dy)
    for dz in range(-2, 3)
    for dx in range(-2, 3)
    for dy in range(-2, 3)
    if abs(dz) + abs(dx) + abs(dy) == 2
)


def rolled(x, offset, axis):
    size = x.shape[axis]
    return pltpu.roll(x, (-offset) % size, axis)


def centre_weight(c):
    return c * ((1.0 / rate - 18.0) + c * (36.0 - 24.0 * c))


def wrap(layer):
    return lax.bitwise_and(layer, LAYERS - 1)


def stencil(ref, layer, row, count):
    here = ref[layer, row : row + count, :]
    return here, (
        ref[wrap(layer + 1), row : row + count, :],
        ref[wrap(layer - 1), row : row + count, :],
        ref[layer, row + 1 : row + 1 + count, :],
        ref[layer, row - 1 : row - 1 + count, :],
        rolled(here, 1, 1),
        rolled(here, -1, 1),
    )


def six(parts):
    return (parts[0] + parts[1]) + (parts[2] + parts[3]) + (parts[4] + parts[5])


def class_sums(labels, weights):
    square = None
    cube = None
    count = len(labels)
    for i in range(count):
        total = weights[i]
        for j in range(i + 1, count):
            total = total + jnp.where(labels[i] == labels[j], weights[j], 0.0)
        rest = total - weights[i]
        both = total + rest
        part2 = weights[i] * both
        part3 = weights[i] * (both * both - total * rest)
        square = part2 if square is None else square + part2
        cube = part3 if cube is None else cube + part3
    return square, cube


def first_sums(lab_ref, c_ref, layer, row, count):
    c, cs = stencil(c_ref, layer, row, count)
    lab, labs = stencil(lab_ref, layer, row, count)
    return (lab,) + labs, (centre_weight(c),) + cs


def kernel(
    where_ref,
    labels_ref,
    dens_ref,
    near_ref,
    far_ref,
    grains_ref,
    out_ref,
    lab,
    c0,
    c1,
    mu,
    k1,
    s2,
    k2,
    lab_copies,
    c_copies,
    w_copies,
    eta_mid,
    eta_edge,
):
    grain = where_ref[0]
    core = lax.rem(grain, 2)
    start = 2 * grain - TILE + LAYERS

    def place(layer, carry):
        z = wrap(start + layer)
        lab[layer, MID : MID + 8, :] = labels_ref[z].astype(jnp.float32)
        c0[layer, MID : MID + 8, :] = dens_ref[z]
        up = 1 - core
        for which, ref in ((0, lab), (1, c0)):
            for block in (0, 1):
                mine = near_ref[which, block, z]
                other = far_ref[which, block, z]
                plus = jnp.where(core == 0, mine, other)
                minus = jnp.where(core == 0, other, mine)
                ref[layer, MID + 8 * (block + 1) : MID + 8 * (block + 2), :] = plus
                ref[layer, MID - 8 * (block + 1) : MID - 8 * block, :] = minus
        return carry

    lax.fori_loop(0, LAYERS, place, 0)

    grain_ids = [(grain * GDEV + g).astype(jnp.float32) for g in range(GDEV)]

    def own_grains(labels, weights):
        result = []
        for g in range(GDEV):
            total = None
            for one, weight in zip(labels, weights):
                part = jnp.where(one == grain_ids[g], weight, 0.0)
                total = part if total is None else total + part
            result.append(rate * total)
        return result

    def store_sums(layer, row, square, cube):
        square = (rate * rate) * square
        k1[layer, row : row + 8, :] = (4.0 * rate**3) * cube - 6.0 * square
        return square

    def sums_all(layer, carry):
        for row in (MID - 8, MID, MID + 8):
            labels, weights = first_sums(lab, c0, layer, row, 8)
            square = store_sums(layer, row, *class_sums(labels, weights))
            s2[layer, row : row + 8, :] = square
            if row == MID:
                for g, value in enumerate(own_grains(labels, weights)):
                    eta_mid[g, layer] = value
        return carry

    lax.fori_loop(0, LAYERS, sums_all, 0)

    def sums_far(layer, carry):
        for row in (MID - 16, MID + 16):
            labels, weights = first_sums(lab, c0, layer, row, 8)
            store_sums(layer, row, *class_sums(labels, weights))
        return carry

    lax.fori_loop(TILE - 6, TILE + 8, sums_far, 0)

    sub = lax.broadcasted_iota(jnp.int32, (8, WIDTH), 0)
    upper = sub < 4

    def edge_grains(layer, carry):
        low_labels, low_weights = first_sums(lab, c0, layer, MID - 8, 8)
        high_labels, high_weights = first_sums(lab, c0, layer, MID + 8, 8)
        labels = [jnp.where(upper, h, w) for h, w in zip(high_labels, low_labels)]
        weights = [jnp.where(upper, h, w) for h, w in zip(high_weights, low_weights)]
        for g, value in enumerate(own_grains(labels, weights)):
            eta_edge[g, layer] = value
        return carry

    lax.fori_loop(0, LAYERS, edge_grains, 0)

    def mu_at(source, extra, layer, row):
        c, cs = stencil(source, layer, row, 8)
        bulk = c * (24.0 + c * (32.0 * c - 48.0)) + extra[layer, row : row + 8, :]
        mu[layer, row : row + 8, :] = bulk - six(cs)

    def c_at(source, layer, row):
        m, ms = stencil(mu, layer, row, 8)
        c = source[layer, row : row + 8, :]
        return c + density_step * (six(ms) - 6.0 * m)

    def over(low, high, rows, body):
        if high > low and rows:

            def step(layer, carry):
                for row in rows:
                    body(layer, row)
                return carry

            lax.fori_loop(low, high, step, 0)

    sides = (MID - 8, MID + 8)
    fars = (MID - 16, MID + 16)

    def near_tile(distance):
        return TILE - distance, TILE + 2 + distance

    for sub_step in range(1, NSUB + 1):
        source = c0 if sub_step == 1 else c1

        def put_mu(layer, row, source=source):
            mu_at(source, k1, layer, row)

        def put_c(layer, row, source=source):
            c1[layer, row : row + 8, :] = c_at(source, layer, row)

        over(0, LAYERS, (MID,) + sides, put_mu)
        if 8 - 2 * sub_step >= 0:
            over(*near_tile(8 - 2 * sub_step), fars, put_mu)
        if sub_step < NSUB:
            over(0, LAYERS, (MID,) + sides, put_c)
            if 7 - 2 * sub_step >= 0:
                over(*near_tile(7 - 2 * sub_step), fars, put_c)
        else:
            over(0, LAYERS, (MID,), put_c)
            over(*near_tile(7), sides, put_c)

    def grain_steps(layer, carry):
        c = c1[layer, MID : MID + 8, :]
        square = s2[layer, MID : MID + 8, :]
        linear = 1.0 - rate * (12.0 * (1.0 - c) + 12.0 * square + 6.0)
        quadratic = (12.0 * rate) * (2.0 - c)
        for g in range(GDEV):
            mid = eta_mid[g, layer]
            edge = eta_edge[g, layer]
            after = jnp.where(sub == 7, rolled(edge, 1, 0), rolled(mid, 1, 0))
            before = jnp.where(sub == 0, rolled(edge, -1, 0), rolled(mid, -1, 0))
            around = six(
                (
                    eta_mid[g, wrap(layer + 1)],
                    eta_mid[g, wrap(layer - 1)],
                    after,
                    before,
                    rolled(mid, 1, 1),
                    rolled(mid, -1, 1),
                )
            )
            grains_ref[g, wrap(start + layer)] = (
                mid * (linear + quadratic * mid) + rate * around
            )
        return carry

    lax.fori_loop(0, LAYERS, grain_steps, 0)

    def copies(index, carry):
        layer = index + BASE
        c_wide = c0[layer, MID - 16 : MID + 24, :]
        lab_wide = lab[layer, MID - 16 : MID + 24, :]
        c_cols = {dy: c_wide if dy == 0 else rolled(c_wide, dy, 1) for dy in range(-2, 3)}
        lab_cols = {dy: lab_wide if dy == 0 else rolled(lab_wide, dy, 1) for dy in range(-2, 3)}
        for slot, (dx, dy) in enumerate(SHIFTS):
            c = c_cols[dy] if dx == 0 else rolled(c_cols[dy], dx, 0)
            one = lab_cols[dy] if dx == 0 else rolled(lab_cols[dy], dx, 0)
            c = c[8:32]
            lab_copies[slot, index] = one[8:32]
            if abs(dx) + abs(dy) < 2:
                w_copies[slot, index] = centre_weight(c)
            c_copies[slot, index] = 2.0 * c if abs(dx) + abs(dy) == 2 and dx * dy else c
        return carry

    lax.fori_loop(0, 20, copies, 0)

    def second_sums(load, c, square):
        labels = [load(lab_copies, cell) for cell in INNER + OUTER]
        first = [load(w_copies, INNER[0])] + [load(c_copies, cell) for cell in INNER[1:]]
        spread = [6.0 * load(c_copies, INNER[0])] + [load(w_copies, cell) for cell in INNER[1:]]
        for cell in OUTER:
            value = load(c_copies, cell)
            if cell[0] in (1, -1):
                value = value + value
            spread.append(value)
        linear = rate - (rate * rate) * (12.0 * (1.0 - c) + 12.0 * square + 6.0)
        quadratic = (12.0 * rate**3) * (2.0 - c)
        inner = None
        outer = None
        for i in range(25):
            total = spread[i]
            own = first[i] if i < 7 else None
            for j in range(i + 1, 25):
                same = labels[i] == labels[j]
                total = total + jnp.where(same, spread[j], 0.0)
                if j < 7:
                    own = own + jnp.where(same, first[j], 0.0)
            rest = total - spread[i]
            if i < 7:
                own_rest = own - first[i]
                value = own * (linear + quadratic * own) + (rate * rate) * total
                value_rest = own_rest * (linear + quadratic * own_rest) + (rate * rate) * rest
                part = value * value * (4.0 * value - 6.0) - value_rest * value_rest * (
                    4.0 * value_rest - 6.0
                )
                inner = part if inner is None else inner + part
            else:
                both = total + rest
                part = spread[i] * (
                    both * ((4.0 * rate * rate) * both - 6.0)
                    - (4.0 * rate * rate) * (total * rest)
                )
                outer = part if outer is None else outer + part
        return inner + (rate**4) * outer

    def load_block(layer, block, lanes):
        def load(ref, cell):
            dz, dx, dy = cell
            return ref[SLOT[dx, dy], layer - BASE + dz, 8 * block : 8 * block + 8, lanes]

        return load

    def halves(low, high, body):
        def step(index, carry):
            lanes = pl.ds(pl.multiple_of(128 * lax.rem(index, 2), 128), 128)
            body(lax.div(index, 2), lanes)
            return carry

        lax.fori_loop(2 * low, 2 * high, step, 0)

    def plain(block):
        row = MID - 8 + 8 * block

        def body(layer, lanes):
            k2[layer, row : row + 8, lanes] = second_sums(
                load_block(layer, block, lanes),
                c1[layer, row : row + 8, lanes],
                s2[layer, row : row + 8, lanes],
            )

        return body

    def merged(layer, lanes):
        high = load_block(layer, 2, lanes)
        low = load_block(layer, 0, lanes)
        pick = lax.broadcasted_iota(jnp.int32, (8, 128), 0) < 4

        def load(ref, cell):
            return jnp.where(pick, high(ref, cell), low(ref, cell))

        value = second_sums(
            load,
            jnp.where(pick, c1[layer, MID + 8 : MID + 16, lanes], c1[layer, MID - 8 : MID, lanes]),
            jnp.where(pick, s2[layer, MID + 8 : MID + 16, lanes], s2[layer, MID - 8 : MID, lanes]),
        )
        k2[layer, MID + 8 : MID + 16, lanes] = value
        k2[layer, MID - 8 : MID, lanes] = value

    halves(TILE - 7, TILE + 9, plain(1))
    halves(TILE - 2, TILE + 4, plain(0))
    halves(TILE - 2, TILE + 4, plain(2))
    halves(TILE - 6, TILE - 2, merged)
    halves(TILE + 4, TILE + 8, merged)

    for sub_step in range(1, NSUB + 1):

        def put_mu(layer, row):
            mu_at(c1, k2, layer, row)

        def put_c(layer, row):
            c1[layer, row : row + 8, :] = c_at(c1, layer, row)

        over(*near_tile(9 - 2 * sub_step), (MID,), put_mu)
        over(*near_tile(8 - 2 * sub_step), sides, put_mu)
        if sub_step < NSUB:
            over(*near_tile(8 - 2 * sub_step), (MID,), put_c)
            over(*near_tile(7 - 2 * sub_step), sides, put_c)
        else:
            for layer in (0, 1):
                out_ref[layer] = c_at(c1, TILE + layer, MID)


def sintering(where, labels, dens, near, far):
    field = pltpu.VMEM((LAYERS, ROWS, WIDTH), jnp.float32)
    vmem = pl.BlockSpec(memory_space=pltpu.VMEM)
    return pl.pallas_call(
        kernel,
        out_shape=(
            jax.ShapeDtypeStruct((GDEV, LAYERS, 8, WIDTH), jnp.float32),
            jax.ShapeDtypeStruct((2, 8, WIDTH), jnp.float32),
        ),
        in_specs=[pl.BlockSpec(memory_space=pltpu.SMEM)] + [vmem] * 4,
        out_specs=(vmem, vmem),
        scratch_shapes=[field] * 7
        + [
            pltpu.VMEM((13, 20, 24, WIDTH), jnp.float32),
            pltpu.VMEM((13, 20, 24, WIDTH), jnp.float32),
            pltpu.VMEM((5, 20, 24, WIDTH), jnp.float32),
            pltpu.VMEM((GDEV, LAYERS, 8, WIDTH), jnp.float32),
            pltpu.VMEM((GDEV, LAYERS, 8, WIDTH), jnp.float32),
        ],
        compiler_params=pltpu.CompilerParams(vmem_limit_bytes=56 * 1024 * 1024),
        name="sintering",
    )(where, labels, dens, near, far)


def from_sides(block, distance):
    grains = lax.axis_size("grain")
    count = lax.axis_size("space")
    pairs = []
    for g in range(grains):
        way = distance if g % 2 == 0 else -distance
        for s in range(count):
            pairs.append((g * count + (s + way) % count, g * count + s))
    return lax.ppermute(block, ("grain", "space"), pairs)


def swap_cores(block):
    return lax.ppermute(block, "grain", [(i, i ^ 1) for i in range(lax.axis_size("grain"))])


def per_device(labels, density):
    grain = lax.axis_index("grain")
    named = labels.astype(jnp.float32)
    own = jnp.broadcast_to(density[None], (lax.axis_size("grain"),) + density.shape)
    dens = lax.all_to_all(own, "grain", 0, 0).reshape(LAYERS, 8, WIDTH)
    named_sides = [from_sides(named, distance) for distance in (1, 2)]
    dens_sides = [from_sides(dens, distance) for distance in (1, 2)]
    near = jnp.stack([jnp.stack(named_sides), jnp.stack(dens_sides)])
    far = swap_cores(near)
    return sintering(grain.reshape(1).astype(jnp.int32), labels, dens, near, far)


def solution(mesh):
    return jax.shard_map(
        per_device,
        mesh=mesh,
        in_specs=(P(None, "space", None), P("grain", "space", None)),
        out_specs=(P("grain", None, "space", None), P("grain", "space", None)),
        check_vma=False,
    )
```

time: 734 us -> 120 us (0.16)
  waiting for transfers between devices: 355 us -> 19.1 us
  starting transfers between devices: 268 us -> 23.7 us
  Pallas kernels: 0 us -> 73 us
  blocking collectives: 52.9 us -> 0 us
  other arithmetic: 19.4 us -> 0.16 us
  local copies, waits for them, and re-layouts: 17.1 us -> 2.47 us
  between operations: 15.1 us -> 0.72 us
    psum x2 -> x0, waiting for transfers between devices: 289 us -> none  [per_device(): square, cube_full = lax.psum((local_square, local_cube), 'grain')]
    ppermute x68 -> x5, starting transfers between devices: 268 us -> 13.4 us  [the longest x4 8.12 us: from_sides(): return lax.ppermute(block, ('grain', 'space'), pairs)]
    pallas_call x0 -> x1, Pallas kernels: none -> 73 us  [sintering(): pl.pallas_call(kernel, out_shape=(jax.ShapeDtypeStruct((GDEV, LAYERS, 8,...]
    all_gather x2 -> x0, blocking collectives: 52.9 us -> none  [per_device(): full_density = lax.all_gather(dens, 'grain', axis=0, tiled=True)]
    ppermute x68 -> x5, waiting for transfers between devices: 65.7 us -> 14.2 us  [the longest x4 12 us: from_sides(): return lax.ppermute(block, ('grain', 'space'), pairs)]
    slice x60 -> x0, local copies, waits for them, and re-layouts: 11.7 us -> none  [the longest x4 5.71 us: order_laplace(): ysum = jnp.roll(inner, 1, 3) + jnp.roll(inner, -1, 3)]
    all_to_all x0 -> x1, starting transfers between devices: none -> 10.3 us  [per_device(): dens = lax.all_to_all(own, 'grain', 0, 0).reshape(LAYERS, 8, WIDTH)]
    sub x8 -> x0, other arithmetic: 7.94 us -> none  [density_steps(): bulk_potential(dens, square_tile, cube_tile)]
  transfers between devices with their start and end apart: 70 -> 6, of which waited for: 31 -> 6; matrix products, arithmetic and copies ran while one was open for 4% -> 0% of each run, Pallas kernels for 0% -> 0%
where the time goes in v1:
time: 120 us; the launch traced here: 119 us
  Pallas kernels  73 us (61%)
  starting transfers between devices  23.7 us (20%)
  waiting for transfers between devices  19.1 us (16%)
  local copies, waits for them, and re-layouts  2.47 us (2%)
    pallas_call x1, Pallas kernels, sintering(): pl.pallas_call(kernel, out_shape=(jax.ShapeDtypeStruct((GDEV, LAYERS, 8,...  73 us
    ppermute x4, waiting for transfers between devices, from_sides(): return lax.ppermute(block, ('grain', 'space'), pairs)  12 us
    all_to_all x1, starting transfers between devices, per_device(): dens = lax.all_to_all(own, 'grain', 0, 0).reshape(LAYERS, 8, WIDTH)  10.3 us
    ppermute x4, starting transfers between devices, from_sides(): return lax.ppermute(block, ('grain', 'space'), pairs)  8.12 us
    ppermute x1, starting transfers between devices, swap_cores(): lax.ppermute(block, 'grain', [(i, i ^ 1) for i in range(lax.axis_size('gr...  5.3 us
    all_to_all x1, waiting for transfers between devices, per_device(): dens = lax.all_to_all(own, 'grain', 0, 0).reshape(LAYERS, 8, WIDTH)  4.83 us
  transfers between devices with their start and end apart: 6, of which 6 were waited for; matrix products, arithmetic and copies ran while one was open for 0% of the time, Pallas kernels for 0%

profile of v1, /device:TPU:1, one launch (start us, length us, event | category | flops | bytes accessed | tf_op | source)
XLA Modules:
  0.0 119.2 jit_solution(10165706723303408360)
XLA Ops:
  0.6 1.4 %broadcast_in_dim.2 = f32[16,2,8,256]{3,2,1,0:T(8,128)} broadcast(f32[2,8,256]{2,1,0:T(8,128)} %param.3), dimensions={1,2,3} | broadcast | bytes 278528 | tf_op jit(solution)/shard_map/broadcast_in_dim | solution.py:432
  2.1 0.0 copy-start.2
  2.1 10.3 %all-to-all-start = ((f32[16,2,8,256]{3,2,1,0:T(8,128)}), f32[16,2,8,256]{3,2,1,0:T(8,128)S(1)}, u32[]{:S(2)}, u32[]{:S(2)}) async-start(f32[16,2,8,256]{3,2,1,0:T(8,128)} %broadcast_in_dim.2), calls=%async_computation | async-start | bytes 524288 | tf_op jit(solution)/shard_map/all_to_all | solution.py:433
  12.4 0.0 copy-done.2
  12.4 1.9 %collective-permute-start.1 = (f32[32,8,256]{2,1,0:T(8,128)S(1)}, f32[32,8,256]{2,1,0:T(8,128)S(1)}, u32[]{:S(2)}, u32[]{:S(2)}) collective-permute-start(f32[32,8,256]{2,1,0:T(8,128)S(1)} %convert_element_type.3), channel_id=1, source_target_pairs={{2,0},{3,1},{4,2},{5,3},{6,4},{7,5},{8,6},{9,7},{10,8},{11,9},{12,... | collective-permute-start | bytes 786440 | tf_op jit(solution)/shard_map/ppermute | solution.py:422
  14.4 2.2 %collective-permute-start = (f32[32,8,256]{2,1,0:T(8,128)S(1)}, f32[32,8,256]{2,1,0:T(8,128)S(1)}, u32[]{:S(2)}, u32[]{:S(2)}) collective-permute-start(f32[32,8,256]{2,1,0:T(8,128)S(1)} %convert_element_type.3), channel_id=1, source_target_pairs={{1,0},{2,1},{3,2},{4,3},{5,4},{6,5},{7,6},{8,7},{9,8},{10,9},{11,1... | collective-permute-start | bytes 786440 | tf_op jit(solution)/shard_map/ppermute | solution.py:422
  16.6 4.8 %all-to-all-done = f32[16,2,8,256]{3,2,1,0:T(8,128)S(1)} async-done(((f32[16,2,8,256]{3,2,1,0:T(8,128)}), f32[16,2,8,256]{3,2,1,0:T(8,128)S(1)}, u32[]{:S(2)}, u32[]{:S(2)}) %all-to-all-start) | async-done | bytes 262176 | tf_op jit(solution)/shard_map/all_to_all | solution.py:433
  21.4 0.0 copy-start.3
  21.4 1.9 %collective-permute-start.3 = (f32[32,8,256]{2,1,0:T(8,128)S(1)}, f32[32,8,256]{2,1,0:T(8,128)S(1)}, u32[]{:S(2)}, u32[]{:S(2)}) collective-permute-start(f32[32,8,256]{2,1,0:T(8,128)S(1)} %bitcast.10), channel_id=1, source_target_pairs={{2,0},{3,1},{4,2},{5,3},{6,4},{7,5},{8,6},{9,7},{10,8},{11,9},{12,... | collective-permute-start | bytes 786440 | tf_op jit(solution)/shard_map/ppermute | solution.py:422
  23.3 2.1 %collective-permute-start.2 = (f32[32,8,256]{2,1,0:T(8,128)S(1)}, f32[32,8,256]{2,1,0:T(8,128)S(1)}, u32[]{:S(2)}, u32[]{:S(2)}) collective-permute-start(f32[32,8,256]{2,1,0:T(8,128)S(1)} %bitcast.11), channel_id=1, source_target_pairs={{1,0},{2,1},{3,2},{4,3},{5,4},{6,5},{7,6},{8,7},{9,8},{10,9},{11,1... | collective-permute-start | bytes 786440 | tf_op jit(solution)/shard_map/ppermute | solution.py:422
  25.4 0.1 collective-permute-done.1
  25.6 3.0 %collective-permute-done = f32[32,8,256]{2,1,0:T(8,128)S(1)} collective-permute-done((f32[32,8,256]{2,1,0:T(8,128)S(1)}, f32[32,8,256]{2,1,0:T(8,128)S(1)}, u32[]{:S(2)}, u32[]{:S(2)}) %collective-permute-start) | collective-permute-done | bytes 262176 | tf_op jit(solution)/shard_map/ppermute | solution.py:422
  28.6 0.0 copy-done.3
  28.6 5.9 %collective-permute-done.3 = f32[32,8,256]{2,1,0:T(8,128)S(1)} collective-permute-done((f32[32,8,256]{2,1,0:T(8,128)S(1)}, f32[32,8,256]{2,1,0:T(8,128)S(1)}, u32[]{:S(2)}, u32[]{:S(2)}) %collective-permute-start.3) | collective-permute-done | bytes 262176 | tf_op jit(solution)/shard_map/ppermute | solution.py:422
  34.5 2.9 %collective-permute-done.2 = f32[32,8,256]{2,1,0:T(8,128)S(1)} collective-permute-done((f32[32,8,256]{2,1,0:T(8,128)S(1)}, f32[32,8,256]{2,1,0:T(8,128)S(1)}, u32[]{:S(2)}, u32[]{:S(2)}) %collective-permute-start.2) | collective-permute-done | bytes 262176 | tf_op jit(solution)/shard_map/ppermute | solution.py:422
  37.5 0.1 pad_maximum_fusion.near_ref
  37.6 0.0 copy-start
  37.6 5.3 %collective-permute-start.4 = (f32[2,2,32,8,256]{4,3,2,1,0:T(8,128)S(1)}, f32[2,2,32,8,256]{4,3,2,1,0:T(8,128)S(1)}, u32[]{:S(2)}, u32[]{:S(2)}) collective-permute-start(f32[2,2,32,8,256]{4,3,2,1,0:T(8,128)S(1)} %pad_maximum_fusion.near_ref), channel_id=1, source_target_pairs={{0,32},{32,0},{64,96},{96,64},{128,160},{160,128},{192,224},{224,1... | collective-permute-start | bytes 3145736 | tf_op jit(solution)/shard_map/ppermute | solution.py:426
  42.9 2.3 %collective-permute-done.4.far_ref = f32[2,2,32,8,256]{4,3,2,1,0:T(8,128)S(1)} collective-permute-done((f32[2,2,32,8,256]{4,3,2,1,0:T(8,128)S(1)}, f32[2,2,32,8,256]{4,3,2,1,0:T(8,128)S(1)}, u32[]{:S(2)}, u32[]{:S(2)}) %collective-permute-start.4) | collective-permute-done | bytes 1048608 | tf_op jit(solution)/shard_map/ppermute | solution.py:426
  45.2 0.0 copy-start.1
  45.2 0.0 copy-done
  45.2 1.0 copy-done.1
  46.2 73.0 %sintering.1 = (f32[4,32,8,256]{3,2,1,0:T(8,128)}, f32[2,8,256]{2,1,0:T(8,128)}) custom-call(s32[1]{0:T(128)} %bitcast.where_ref, s32[32,8,256]{2,1,0:T(8,128)} %labels_ref.1, f32[32,8,256]{2,1,0:T(8,128)} %bitcast.12, f32[2,2,32,8,256]{4,3,2,1,0:T(8,128)} %copy-done, f32[2,2,32,8,256]{4,3,2,1,0:T(8,128)} %copy-done.1), custom_call_target="tpu_custom_call" | custom-call | tf_op jit(solution)/shard_map/sintering/pallas_call | solution.py:393
  (3 shorter events, 0.1 us)
Async XLA Ops:
  2.1 10.3 %copy-start.2 = (s32[32,8,256]{2,1,0:T(8,128)S(1)}, s32[32,8,256]{2,1,0:T(8,128)}, u32[]{:S(2)}) copy-start(s32[32,8,256]{2,1,0:T(8,128)} %labels_ref.1) | copy-start | bytes 786436
  2.1 19.3 %all-to-all-start = ((f32[16,2,8,256]{3,2,1,0:T(8,128)}), f32[16,2,8,256]{3,2,1,0:T(8,128)S(1)}, u32[]{:S(2)}, u32[]{:S(2)}) async-start(f32[16,2,8,256]{3,2,1,0:T(8,128)} %broadcast_in_dim.2), calls=%async_computation | async-start | bytes 524288 | tf_op jit(solution)/shard_map/all_to_all | solution.py:433
  12.4 13.1 %collective-permute-start.1 = (f32[32,8,256]{2,1,0:T(8,128)S(1)}, f32[32,8,256]{2,1,0:T(8,128)S(1)}, u32[]{:S(2)}, u32[]{:S(2)}) collective-permute-start(f32[32,8,256]{2,1,0:T(8,128)S(1)} %convert_element_type.3), channel_id=1, source_target_pairs={{2,0},{3,1},{4,2},{5,3},{6,4},{7,5},{8,6},{9,7},{10,8},{11,9},{12,... | collective-permute-start | bytes 786440 | tf_op jit(solution)/shard_map/ppermute | solution.py:422
  14.4 14.2 %collective-permute-start = (f32[32,8,256]{2,1,0:T(8,128)S(1)}, f32[32,8,256]{2,1,0:T(8,128)S(1)}, u32[]{:S(2)}, u32[]{:S(2)}) collective-permute-start(f32[32,8,256]{2,1,0:T(8,128)S(1)} %convert_element_type.3), channel_id=1, source_target_pairs={{1,0},{2,1},{3,2},{4,3},{5,4},{6,5},{7,6},{8,7},{9,8},{10,9},{11,1... | collective-permute-start | bytes 786440 | tf_op jit(solution)/shard_map/ppermute | solution.py:422
  21.4 7.2 %copy-start.3 = (f32[16,2,8,256]{3,2,1,0:T(8,128)}, f32[16,2,8,256]{3,2,1,0:T(8,128)S(1)}, u32[]{:S(2)}) copy-start(f32[16,2,8,256]{3,2,1,0:T(8,128)S(1)} %all-to-all-done) | copy-start | bytes 786436
  21.4 13.1 %collective-permute-start.3 = (f32[32,8,256]{2,1,0:T(8,128)S(1)}, f32[32,8,256]{2,1,0:T(8,128)S(1)}, u32[]{:S(2)}, u32[]{:S(2)}) collective-permute-start(f32[32,8,256]{2,1,0:T(8,128)S(1)} %bitcast.10), channel_id=1, source_target_pairs={{2,0},{3,1},{4,2},{5,3},{6,4},{7,5},{8,6},{9,7},{10,8},{11,9},{12,... | collective-permute-start | bytes 786440 | tf_op jit(solution)/shard_map/ppermute | solution.py:422
  23.3 14.2 %collective-permute-start.2 = (f32[32,8,256]{2,1,0:T(8,128)S(1)}, f32[32,8,256]{2,1,0:T(8,128)S(1)}, u32[]{:S(2)}, u32[]{:S(2)}) collective-permute-start(f32[32,8,256]{2,1,0:T(8,128)S(1)} %bitcast.11), channel_id=1, source_target_pairs={{1,0},{2,1},{3,2},{4,3},{5,4},{6,5},{7,6},{8,7},{9,8},{10,9},{11,1... | collective-permute-start | bytes 786440 | tf_op jit(solution)/shard_map/ppermute | solution.py:422
  37.6 7.6 %copy-start = (f32[2,2,32,8,256]{4,3,2,1,0:T(8,128)}, f32[2,2,32,8,256]{4,3,2,1,0:T(8,128)S(1)}, u32[]{:S(2)}) copy-start(f32[2,2,32,8,256]{4,3,2,1,0:T(8,128)S(1)} %pad_maximum_fusion.near_ref) | copy-start | bytes 3145732
  37.6 7.6 %collective-permute-start.4 = (f32[2,2,32,8,256]{4,3,2,1,0:T(8,128)S(1)}, f32[2,2,32,8,256]{4,3,2,1,0:T(8,128)S(1)}, u32[]{:S(2)}, u32[]{:S(2)}) collective-permute-start(f32[2,2,32,8,256]{4,3,2,1,0:T(8,128)S(1)} %pad_maximum_fusion.near_ref), channel_id=1, source_target_pairs={{0,32},{32,0},{64,96},{96,64},{128,160},{160,128},{192,224},{224,1... | collective-permute-start | bytes 3145736 | tf_op jit(solution)/shard_map/ppermute | solution.py:426
  45.2 1.0 copy-start.1

commit v2 on v1

--- a/solution.py
+++ b/solution.py
@@ -10,11 +10,13 @@
 GDEV = 4
 NSUB = 4
 LAYERS = 32
+DEEP = 34
 WIDTH = 256
 ROWS = 56
 MID = 24
-TILE = 15
-BASE = 6
+TILE = 16
+BASE = 7
+GROUP = 4
 
 rate = 0.008 * 2.0
 density_step = 0.004
@@ -61,8 +63,8 @@
 def stencil(ref, layer, row, count):
     here = ref[layer, row : row + count, :]
     return here, (
-        ref[wrap(layer + 1), row : row + count, :],
-        ref[wrap(layer - 1), row : row + count, :],
+        ref[layer + 1, row : row + count, :],
+        ref[layer - 1, row : row + count, :],
         ref[layer, row + 1 : row + 1 + count, :],
         ref[layer, row - 1 : row - 1 + count, :],
         rolled(here, 1, 1),
@@ -97,6 +99,24 @@
     return (lab,) + labs, (centre_weight(c),) + cs
 
 
+def chunks(low, high, body, group):
+    count = high - low
+    while count % group:
+        group -= 1
+
+    def step(index, carry):
+        for k in range(group):
+            body(low + index * group + k)
+        return carry
+
+    lax.fori_loop(0, count // group, step, 0)
+
+
+def close_ends(ref, rows):
+    ref[0, rows, :] = ref[LAYERS, rows, :]
+    ref[LAYERS + 1, rows, :] = ref[1, rows, :]
+
+
 def kernel(
     where_ref,
     labels_ref,
@@ -108,6 +128,7 @@
     lab,
     c0,
     c1,
+    cx,
     mu,
     k1,
     s2,
@@ -122,7 +143,7 @@
     core = lax.rem(grain, 2)
     start = 2 * grain - TILE + LAYERS
 
-    def place(layer, carry):
+    def place(layer):
         z = wrap(start + layer)
         lab[layer, MID : MID + 8, :] = labels_ref[z].astype(jnp.float32)
         c0[layer, MID : MID + 8, :] = dens_ref[z]
@@ -135,9 +156,8 @@
                 minus = jnp.where(core == 0, other, mine)
                 ref[layer, MID + 8 * (block + 1) : MID + 8 * (block + 2), :] = plus
                 ref[layer, MID - 8 * (block + 1) : MID - 8 * block, :] = minus
-        return carry
-
-    lax.fori_loop(0, LAYERS, place, 0)
+
+    chunks(0, DEEP, place, 2)
 
     grain_ids = [(grain * GDEV + g).astype(jnp.float32) for g in range(GDEV)]
 
@@ -156,7 +176,7 @@
         k1[layer, row : row + 8, :] = (4.0 * rate**3) * cube - 6.0 * square
         return square
 
-    def sums_all(layer, carry):
+    def sums_all(layer):
         for row in (MID - 8, MID, MID + 8):
             labels, weights = first_sums(lab, c0, layer, row, 8)
             square = store_sums(layer, row, *class_sums(labels, weights))
@@ -164,31 +184,47 @@
             if row == MID:
                 for g, value in enumerate(own_grains(labels, weights)):
                     eta_mid[g, layer] = value
-        return carry
-
-    lax.fori_loop(0, LAYERS, sums_all, 0)
-
-    def sums_far(layer, carry):
+
+    chunks(1, LAYERS + 1, sums_all, 1)
+    for g in range(GDEV):
+        eta_mid[g, 0] = eta_mid[g, LAYERS]
+        eta_mid[g, LAYERS + 1] = eta_mid[g, 1]
+
+    def sums_far(layer):
         for row in (MID - 16, MID + 16):
             labels, weights = first_sums(lab, c0, layer, row, 8)
             store_sums(layer, row, *class_sums(labels, weights))
-        return carry
-
-    lax.fori_loop(TILE - 6, TILE + 8, sums_far, 0)
+
+    chunks(TILE - 6, TILE + 8, sums_far, 1)
 
     sub = lax.broadcasted_iota(jnp.int32, (8, WIDTH), 0)
     upper = sub < 4
 
-    def edge_grains(layer, carry):
-        low_labels, low_weights = first_sums(lab, c0, layer, MID - 8, 8)
-        high_labels, high_weights = first_sums(lab, c0, layer, MID + 8, 8)
-        labels = [jnp.where(upper, h, w) for h, w in zip(high_labels, low_labels)]
-        weights = [jnp.where(upper, h, w) for h, w in zip(high_weights, low_weights)]
-        for g, value in enumerate(own_grains(labels, weights)):
+    def edge_stencil(ref, layer):
+        def both(z, offset):
+            return jnp.where(
+                upper,
+                ref[z, MID + 8 + offset : MID + 16 + offset, :],
+                ref[z, MID - 8 + offset : MID + offset, :],
+            )
+
+        here = both(layer, 0)
+        return here, (
+            both(layer + 1, 0),
+            both(layer - 1, 0),
+            both(layer, 1),
+            both(layer, -1),
+            rolled(here, 1, 1),
+            rolled(here, -1, 1),
+        )
+
+    def edge_grains(layer):
+        c, cs = edge_stencil(c0, layer)
+        one, ones = edge_stencil(lab, layer)
+        for g, value in enumerate(own_grains((one,) + ones, (centre_weight(c),) + cs)):
             eta_edge[g, layer] = value
-        return carry
-
-    lax.fori_loop(0, LAYERS, edge_grains, 0)
+
+    chunks(1, LAYERS + 1, edge_grains, 2)
 
     def mu_at(source, extra, layer, row):
         c, cs = stencil(source, layer, row, 8)
@@ -203,12 +239,11 @@
     def over(low, high, rows, body):
         if high > low and rows:
 
-            def step(layer, carry):
+            def step(layer):
                 for row in rows:
                     body(layer, row)
-                return carry
-
-            lax.fori_loop(low, high, step, 0)
+
+            chunks(low, high, step, GROUP if len(rows) > 1 else 2 * GROUP)
 
     sides = (MID - 8, MID + 8)
     fars = (MID - 16, MID + 16)
@@ -216,27 +251,31 @@
     def near_tile(distance):
         return TILE - distance, TILE + 2 + distance
 
+    near_rows = slice(MID - 8, MID + 16)
     for sub_step in range(1, NSUB + 1):
-        source = c0 if sub_step == 1 else c1
+        source = c0 if sub_step == 1 else (cx, c1)[sub_step % 2]
+        target = (c1, cx)[sub_step % 2]
 
         def put_mu(layer, row, source=source):
             mu_at(source, k1, layer, row)
 
-        def put_c(layer, row, source=source):
-            c1[layer, row : row + 8, :] = c_at(source, layer, row)
-
-        over(0, LAYERS, (MID,) + sides, put_mu)
+        def put_c(layer, row, source=source, target=target):
+            target[layer, row : row + 8, :] = c_at(source, layer, row)
+
+        over(1, LAYERS + 1, (MID,) + sides, put_mu)
+        close_ends(mu, near_rows)
         if 8 - 2 * sub_step >= 0:
             over(*near_tile(8 - 2 * sub_step), fars, put_mu)
         if sub_step < NSUB:
-            over(0, LAYERS, (MID,) + sides, put_c)
+            over(1, LAYERS + 1, (MID,) + sides, put_c)
+            close_ends(target, near_rows)
             if 7 - 2 * sub_step >= 0:
                 over(*near_tile(7 - 2 * sub_step), fars, put_c)
         else:
-            over(0, LAYERS, (MID,), put_c)
+            over(1, LAYERS + 1, (MID,), put_c)
             over(*near_tile(7), sides, put_c)
 
-    def grain_steps(layer, carry):
+    def grain_steps(layer):
         c = c1[layer, MID : MID + 8, :]
         square = s2[layer, MID : MID + 8, :]
         linear = 1.0 - rate * (12.0 * (1.0 - c) + 12.0 * square + 6.0)
@@ -248,8 +287,8 @@
             before = jnp.where(sub == 0, rolled(edge, -1, 0), rolled(mid, -1, 0))
             around = six(
                 (
-                    eta_mid[g, wrap(layer + 1)],
-                    eta_mid[g, wrap(layer - 1)],
+                    eta_mid[g, layer + 1],
+                    eta_mid[g, layer - 1],
                     after,
                     before,
                     rolled(mid, 1, 1),
@@ -259,11 +298,10 @@
             grains_ref[g, wrap(start + layer)] = (
                 mid * (linear + quadratic * mid) + rate * around
             )
-        return carry
-
-    lax.fori_loop(0, LAYERS, grain_steps, 0)
-
-    def copies(index, carry):
+
+    chunks(1, LAYERS + 1, grain_steps, 2)
+
+    def copies(index):
         layer = index + BASE
         c_wide = c0[layer, MID - 16 : MID + 24, :]
         lab_wide = lab[layer, MID - 16 : MID + 24, :]
@@ -277,9 +315,8 @@
             if abs(dx) + abs(dy) < 2:
                 w_copies[slot, index] = centre_weight(c)
             c_copies[slot, index] = 2.0 * c if abs(dx) + abs(dy) == 2 and dx * dy else c
-        return carry
-
-    lax.fori_loop(0, 20, copies, 0)
+
+    chunks(0, 20, copies, 1)
 
     def second_sums(load, c, square):
         labels = [load(lab_copies, cell) for cell in INNER + OUTER]
@@ -370,12 +407,14 @@
     halves(TILE + 4, TILE + 8, merged)
 
     for sub_step in range(1, NSUB + 1):
-
-        def put_mu(layer, row):
-            mu_at(c1, k2, layer, row)
-
-        def put_c(layer, row):
-            c1[layer, row : row + 8, :] = c_at(c1, layer, row)
+        source = (cx, c1)[sub_step % 2]
+        target = (c1, cx)[sub_step % 2]
+
+        def put_mu(layer, row, source=source):
+            mu_at(source, k2, layer, row)
+
+        def put_c(layer, row, source=source, target=target):
+            target[layer, row : row + 8, :] = c_at(source, layer, row)
 
         over(*near_tile(9 - 2 * sub_step), (MID,), put_mu)
         over(*near_tile(8 - 2 * sub_step), sides, put_mu)
@@ -384,11 +423,11 @@
             over(*near_tile(7 - 2 * sub_step), sides, put_c)
         else:
             for layer in (0, 1):
-                out_ref[layer] = c_at(c1, TILE + layer, MID)
+                out_ref[layer] = c_at(source, TILE + layer, MID)
 
 
 def sintering(where, labels, dens, near, far):
-    field = pltpu.VMEM((LAYERS, ROWS, WIDTH), jnp.float32)
+    field = pltpu.VMEM((DEEP, ROWS, WIDTH), jnp.float32)
     vmem = pl.BlockSpec(memory_space=pltpu.VMEM)
     return pl.pallas_call(
         kernel,
@@ -398,13 +437,13 @@
         ),
         in_specs=[pl.BlockSpec(memory_space=pltpu.SMEM)] + [vmem] * 4,
         out_specs=(vmem, vmem),
-        scratch_shapes=[field] * 7
+        scratch_shapes=[field] * 8
         + [
             pltpu.VMEM((13, 20, 24, WIDTH), jnp.float32),
             pltpu.VMEM((13, 20, 24, WIDTH), jnp.float32),
             pltpu.VMEM((5, 20, 24, WIDTH), jnp.float32),
-            pltpu.VMEM((GDEV, LAYERS, 8, WIDTH), jnp.float32),
-            pltpu.VMEM((GDEV, LAYERS, 8, WIDTH), jnp.float32),
+            pltpu.VMEM((GDEV, DEEP, 8, WIDTH), jnp.float32),
+            pltpu.VMEM((GDEV, DEEP, 8, WIDTH), jnp.float32),
         ],
         compiler_params=pltpu.CompilerParams(vmem_limit_bytes=56 * 1024 * 1024),
         name="sintering",

time: 120 us -> 92 us (0.77)
  Pallas kernels: 73 us -> 45.4 us
    pallas_call x1, Pallas kernels: 73 us -> 45.4 us  [sintering(): pl.pallas_call(kernel, out_shape=(jax.ShapeDtypeStruct((GDEV, LAYERS, 8,...]
where the time goes in v2:
time: 92 us; the launch traced here: 91.6 us
  Pallas kernels  45.4 us (49%)
  starting transfers between devices  23.7 us (26%)
  waiting for transfers between devices  19.1 us (21%)
  local copies, waits for them, and re-layouts  2.47 us (3%)
    pallas_call x1, Pallas kernels, sintering(): pl.pallas_call(kernel, out_shape=(jax.ShapeDtypeStruct((GDEV, LAYERS, 8,...  45.4 us
    ppermute x4, waiting for transfers between devices, from_sides(): return lax.ppermute(block, ('grain', 'space'), pairs)  12 us
    all_to_all x1, starting transfers between devices, per_device(): dens = lax.all_to_all(own, 'grain', 0, 0).reshape(LAYERS, 8, WIDTH)  10.3 us
    ppermute x4, starting transfers between devices, from_sides(): return lax.ppermute(block, ('grain', 'space'), pairs)  8.12 us
    ppermute x1, starting transfers between devices, swap_cores(): lax.ppermute(block, 'grain', [(i, i ^ 1) for i in range(lax.axis_size('gr...  5.3 us
    all_to_all x1, waiting for transfers between devices, per_device(): dens = lax.all_to_all(own, 'grain', 0, 0).reshape(LAYERS, 8, WIDTH)  4.83 us
    ppermute x1, waiting for transfers between devices, swap_cores(): lax.ppermute(block, 'grain', [(i, i ^ 1) for i in range(lax.axis_size('gr...  2.26 us
  transfers between devices with their start and end apart: 6, of which 6 were waited for; matrix products, arithmetic and copies ran while one was open for 0% of the time, Pallas kernels for 0%

profile of v2, /device:TPU:1, one launch (start us, length us, event | category | flops | bytes accessed | tf_op | source)
XLA Modules:
  0.0 91.6 jit_solution(15005594795341781214)
XLA Ops:
  0.6 1.4 %broadcast_in_dim.2 = f32[16,2,8,256]{3,2,1,0:T(8,128)} broadcast(f32[2,8,256]{2,1,0:T(8,128)} %param.3), dimensions={1,2,3} | broadcast | bytes 278528 | tf_op jit(solution)/shard_map/broadcast_in_dim | solution.py:471
  2.1 0.0 copy-start.2
  2.1 10.3 %all-to-all-start = ((f32[16,2,8,256]{3,2,1,0:T(8,128)}), f32[16,2,8,256]{3,2,1,0:T(8,128)S(1)}, u32[]{:S(2)}, u32[]{:S(2)}) async-start(f32[16,2,8,256]{3,2,1,0:T(8,128)} %broadcast_in_dim.2), calls=%async_computation | async-start | bytes 524288 | tf_op jit(solution)/shard_map/all_to_all | solution.py:472
  12.4 0.0 copy-done.2
  12.4 1.9 %collective-permute-start.1 = (f32[32,8,256]{2,1,0:T(8,128)S(1)}, f32[32,8,256]{2,1,0:T(8,128)S(1)}, u32[]{:S(2)}, u32[]{:S(2)}) collective-permute-start(f32[32,8,256]{2,1,0:T(8,128)S(1)} %convert_element_type.3), channel_id=1, source_target_pairs={{2,0},{3,1},{4,2},{5,3},{6,4},{7,5},{8,6},{9,7},{10,8},{11,9},{12,... | collective-permute-start | bytes 786440 | tf_op jit(solution)/shard_map/ppermute | solution.py:461
  14.4 2.2 %collective-permute-start = (f32[32,8,256]{2,1,0:T(8,128)S(1)}, f32[32,8,256]{2,1,0:T(8,128)S(1)}, u32[]{:S(2)}, u32[]{:S(2)}) collective-permute-start(f32[32,8,256]{2,1,0:T(8,128)S(1)} %convert_element_type.3), channel_id=1, source_target_pairs={{1,0},{2,1},{3,2},{4,3},{5,4},{6,5},{7,6},{8,7},{9,8},{10,9},{11,1... | collective-permute-start | bytes 786440 | tf_op jit(solution)/shard_map/ppermute | solution.py:461
  16.6 4.8 %all-to-all-done = f32[16,2,8,256]{3,2,1,0:T(8,128)S(1)} async-done(((f32[16,2,8,256]{3,2,1,0:T(8,128)}), f32[16,2,8,256]{3,2,1,0:T(8,128)S(1)}, u32[]{:S(2)}, u32[]{:S(2)}) %all-to-all-start) | async-done | bytes 262176 | tf_op jit(solution)/shard_map/all_to_all | solution.py:472
  21.4 0.0 copy-start.3
  21.4 1.9 %collective-permute-start.3 = (f32[32,8,256]{2,1,0:T(8,128)S(1)}, f32[32,8,256]{2,1,0:T(8,128)S(1)}, u32[]{:S(2)}, u32[]{:S(2)}) collective-permute-start(f32[32,8,256]{2,1,0:T(8,128)S(1)} %bitcast.10), channel_id=1, source_target_pairs={{2,0},{3,1},{4,2},{5,3},{6,4},{7,5},{8,6},{9,7},{10,8},{11,9},{12,... | collective-permute-start | bytes 786440 | tf_op jit(solution)/shard_map/ppermute | solution.py:461
  23.3 2.1 %collective-permute-start.2 = (f32[32,8,256]{2,1,0:T(8,128)S(1)}, f32[32,8,256]{2,1,0:T(8,128)S(1)}, u32[]{:S(2)}, u32[]{:S(2)}) collective-permute-start(f32[32,8,256]{2,1,0:T(8,128)S(1)} %bitcast.11), channel_id=1, source_target_pairs={{1,0},{2,1},{3,2},{4,3},{5,4},{6,5},{7,6},{8,7},{9,8},{10,9},{11,1... | collective-permute-start | bytes 786440 | tf_op jit(solution)/shard_map/ppermute | solution.py:461
  25.4 0.1 collective-permute-done.1
  25.6 3.0 %collective-permute-done = f32[32,8,256]{2,1,0:T(8,128)S(1)} collective-permute-done((f32[32,8,256]{2,1,0:T(8,128)S(1)}, f32[32,8,256]{2,1,0:T(8,128)S(1)}, u32[]{:S(2)}, u32[]{:S(2)}) %collective-permute-start) | collective-permute-done | bytes 262176 | tf_op jit(solution)/shard_map/ppermute | solution.py:461
  28.6 0.0 copy-done.3
  28.6 5.9 %collective-permute-done.3 = f32[32,8,256]{2,1,0:T(8,128)S(1)} collective-permute-done((f32[32,8,256]{2,1,0:T(8,128)S(1)}, f32[32,8,256]{2,1,0:T(8,128)S(1)}, u32[]{:S(2)}, u32[]{:S(2)}) %collective-permute-start.3) | collective-permute-done | bytes 262176 | tf_op jit(solution)/shard_map/ppermute | solution.py:461
  34.5 2.9 %collective-permute-done.2 = f32[32,8,256]{2,1,0:T(8,128)S(1)} collective-permute-done((f32[32,8,256]{2,1,0:T(8,128)S(1)}, f32[32,8,256]{2,1,0:T(8,128)S(1)}, u32[]{:S(2)}, u32[]{:S(2)}) %collective-permute-start.2) | collective-permute-done | bytes 262176 | tf_op jit(solution)/shard_map/ppermute | solution.py:461
  37.5 0.1 pad_maximum_fusion.near_ref
  37.6 0.0 copy-start
  37.6 5.3 %collective-permute-start.4 = (f32[2,2,32,8,256]{4,3,2,1,0:T(8,128)S(1)}, f32[2,2,32,8,256]{4,3,2,1,0:T(8,128)S(1)}, u32[]{:S(2)}, u32[]{:S(2)}) collective-permute-start(f32[2,2,32,8,256]{4,3,2,1,0:T(8,128)S(1)} %pad_maximum_fusion.near_ref), channel_id=1, source_target_pairs={{0,32},{32,0},{64,96},{96,64},{128,160},{160,128},{192,224},{224,1... | collective-permute-start | bytes 3145736 | tf_op jit(solution)/shard_map/ppermute | solution.py:465
  42.9 2.3 %collective-permute-done.4.far_ref = f32[2,2,32,8,256]{4,3,2,1,0:T(8,128)S(1)} collective-permute-done((f32[2,2,32,8,256]{4,3,2,1,0:T(8,128)S(1)}, f32[2,2,32,8,256]{4,3,2,1,0:T(8,128)S(1)}, u32[]{:S(2)}, u32[]{:S(2)}) %collective-permute-start.4) | collective-permute-done | bytes 1048608 | tf_op jit(solution)/shard_map/ppermute | solution.py:465
  45.2 0.0 copy-start.1
  45.2 0.0 copy-done
  45.2 1.0 %copy-done.1 = f32[2,2,32,8,256]{4,3,2,1,0:T(8,128)} copy-done((f32[2,2,32,8,256]{4,3,2,1,0:T(8,128)}, f32[2,2,32,8,256]{4,3,2,1,0:T(8,128)S(1)}, u32[]{:S(2)}) %copy-start.1) | copy-done | bytes 1048600
  46.2 45.4 %sintering.1 = (f32[4,32,8,256]{3,2,1,0:T(8,128)}, f32[2,8,256]{2,1,0:T(8,128)}) custom-call(s32[1]{0:T(128)} %bitcast.where_ref, s32[32,8,256]{2,1,0:T(8,128)} %labels_ref.1, f32[32,8,256]{2,1,0:T(8,128)} %bitcast.12, f32[2,2,32,8,256]{4,3,2,1,0:T(8,128)} %copy-done, f32[2,2,32,8,256]{4,3,2,1,0:T(8,128)} %copy-done.1), custom_call_target="tpu_custom_call" | custom-call | tf_op jit(solution)/shard_map/sintering/pallas_call | solution.py:432
  (3 shorter events, 0.1 us)
Async XLA Ops:
  2.1 10.3 %copy-start.2 = (s32[32,8,256]{2,1,0:T(8,128)S(1)}, s32[32,8,256]{2,1,0:T(8,128)}, u32[]{:S(2)}) copy-start(s32[32,8,256]{2,1,0:T(8,128)} %labels_ref.1) | copy-start | bytes 786436
  2.1 19.3 %all-to-all-start = ((f32[16,2,8,256]{3,2,1,0:T(8,128)}), f32[16,2,8,256]{3,2,1,0:T(8,128)S(1)}, u32[]{:S(2)}, u32[]{:S(2)}) async-start(f32[16,2,8,256]{3,2,1,0:T(8,128)} %broadcast_in_dim.2), calls=%async_computation | async-start | bytes 524288 | tf_op jit(solution)/shard_map/all_to_all | solution.py:472
  12.4 13.1 %collective-permute-start.1 = (f32[32,8,256]{2,1,0:T(8,128)S(1)}, f32[32,8,256]{2,1,0:T(8,128)S(1)}, u32[]{:S(2)}, u32[]{:S(2)}) collective-permute-start(f32[32,8,256]{2,1,0:T(8,128)S(1)} %convert_element_type.3), channel_id=1, source_target_pairs={{2,0},{3,1},{4,2},{5,3},{6,4},{7,5},{8,6},{9,7},{10,8},{11,9},{12,... | collective-permute-start | bytes 786440 | tf_op jit(solution)/shard_map/ppermute | solution.py:461
  14.4 14.2 %collective-permute-start = (f32[32,8,256]{2,1,0:T(8,128)S(1)}, f32[32,8,256]{2,1,0:T(8,128)S(1)}, u32[]{:S(2)}, u32[]{:S(2)}) collective-permute-start(f32[32,8,256]{2,1,0:T(8,128)S(1)} %convert_element_type.3), channel_id=1, source_target_pairs={{1,0},{2,1},{3,2},{4,3},{5,4},{6,5},{7,6},{8,7},{9,8},{10,9},{11,1... | collective-permute-start | bytes 786440 | tf_op jit(solution)/shard_map/ppermute | solution.py:461
  21.4 7.2 %copy-start.3 = (f32[16,2,8,256]{3,2,1,0:T(8,128)}, f32[16,2,8,256]{3,2,1,0:T(8,128)S(1)}, u32[]{:S(2)}) copy-start(f32[16,2,8,256]{3,2,1,0:T(8,128)S(1)} %all-to-all-done) | copy-start | bytes 786436
  21.4 13.1 %collective-permute-start.3 = (f32[32,8,256]{2,1,0:T(8,128)S(1)}, f32[32,8,256]{2,1,0:T(8,128)S(1)}, u32[]{:S(2)}, u32[]{:S(2)}) collective-permute-start(f32[32,8,256]{2,1,0:T(8,128)S(1)} %bitcast.10), channel_id=1, source_target_pairs={{2,0},{3,1},{4,2},{5,3},{6,4},{7,5},{8,6},{9,7},{10,8},{11,9},{12,... | collective-permute-start | bytes 786440 | tf_op jit(solution)/shard_map/ppermute | solution.py:461
  23.3 14.2 %collective-permute-start.2 = (f32[32,8,256]{2,1,0:T(8,128)S(1)}, f32[32,8,256]{2,1,0:T(8,128)S(1)}, u32[]{:S(2)}, u32[]{:S(2)}) collective-permute-start(f32[32,8,256]{2,1,0:T(8,128)S(1)} %bitcast.11), channel_id=1, source_target_pairs={{1,0},{2,1},{3,2},{4,3},{5,4},{6,5},{7,6},{8,7},{9,8},{10,9},{11,1... | collective-permute-start | bytes 786440 | tf_op jit(solution)/shard_map/ppermute | solution.py:461
  37.6 7.6 %copy-start = (f32[2,2,32,8,256]{4,3,2,1,0:T(8,128)}, f32[2,2,32,8,256]{4,3,2,1,0:T(8,128)S(1)}, u32[]{:S(2)}) copy-start(f32[2,2,32,8,256]{4,3,2,1,0:T(8,128)S(1)} %pad_maximum_fusion.near_ref) | copy-start | bytes 3145732
  37.6 7.6 %collective-permute-start.4 = (f32[2,2,32,8,256]{4,3,2,1,0:T(8,128)S(1)}, f32[2,2,32,8,256]{4,3,2,1,0:T(8,128)S(1)}, u32[]{:S(2)}, u32[]{:S(2)}) collective-permute-start(f32[2,2,32,8,256]{4,3,2,1,0:T(8,128)S(1)} %pad_maximum_fusion.near_ref), channel_id=1, source_target_pairs={{0,32},{32,0},{64,96},{96,64},{128,160},{160,128},{192,224},{224,1... | collective-permute-start | bytes 3145736 | tf_op jit(solution)/shard_map/ppermute | solution.py:465
  45.2 1.0 %copy-start.1 = (f32[2,2,32,8,256]{4,3,2,1,0:T(8,128)}, f32[2,2,32,8,256]{4,3,2,1,0:T(8,128)S(1)}, u32[]{:S(2)}) copy-start(f32[2,2,32,8,256]{4,3,2,1,0:T(8,128)S(1)} %collective-permute-done.4.far_ref) | copy-start | bytes 3145732

commit v3 on v2

v3 whole, which is shorter than its diff:
```python
import functools

import jax
import jax.numpy as jnp
from jax import lax
from jax.experimental import pallas as pl
from jax.experimental.pallas import tpu as pltpu
from jax.sharding import PartitionSpec as P

GDEV = 4
NSUB = 4
LAYERS = 32
DEEP = 34
WIDTH = 256
HALF = 128
ROWS = 56
MID = 24
TILE = 16
BASE = 7
GROUP = 32

rate = 0.008 * 2.0
density_step = 0.004

INNER = ((0, 0, 0), (1, 0, 0), (-1, 0, 0), (0, 1, 0), (0, -1, 0), (0, 0, 1), (0, 0, -1))
OUTER = tuple(
    (dz, dx, dy)
    for dz in range(-2, 3)
    for dx in range(-2, 3)
    for dy in range(-2, 3)
    if abs(dz) + abs(dx) + abs(dy) == 2
)


def rolled(x, offset, axis):
    size = x.shape[axis]
    return pltpu.roll(x, (-offset) % size, axis)


def along(pair, offset):
    left, right = rolled(pair[0], offset, 1), rolled(pair[1], offset, 1)
    lane = lax.broadcasted_iota(jnp.int32, left.shape, 1)
    if offset > 0:
        same = lane < HALF - offset
    else:
        same = lane >= -offset
    return jnp.where(same, left, right), jnp.where(same, right, left)


def centre_weight(c):
    return c * ((1.0 / rate - 18.0) + c * (36.0 - 24.0 * c))


def wrap(layer):
    return lax.bitwise_and(layer, LAYERS - 1)


def halves_of(ref, layer, row, count=8):
    return tuple(ref[layer, half, row : row + count, :] for half in range(2))


def stencil(ref, layer, row, count=8):
    here = halves_of(ref, layer, row, count)
    return (
        here,
        halves_of(ref, layer + 1, row, count),
        halves_of(ref, layer - 1, row, count),
        halves_of(ref, layer, row + 1, count),
        halves_of(ref, layer, row - 1, count),
        along(here, 1),
        along(here, -1),
    )


def six(parts):
    return (parts[0] + parts[1]) + (parts[2] + parts[3]) + (parts[4] + parts[5])


def plus(total, part):
    return part if total is None else total + part


def class_sums(labels, weights):
    square = None
    cube = None
    count = len(labels)
    for i in range(count):
        rest = None
        for j in range(i + 1, count):
            rest = plus(rest, jnp.where(labels[i] == labels[j], weights[j], 0.0))
        if rest is None:
            part2 = weights[i] * weights[i]
            part3 = part2 * weights[i]
        else:
            total = rest + weights[i]
            both = total + rest
            part2 = weights[i] * both
            part3 = weights[i] * (both * both - total * rest)
        square = plus(square, part2)
        cube = plus(cube, part3)
    return square, cube


def chunks(low, high, body, group):
    count = high - low
    while count % group:
        group -= 1

    def step(index, carry):
        for k in range(group):
            body(low + index * group + k)
        return carry

    lax.fori_loop(0, count // group, step, 0)


def close_ends(ref, rows):
    ref[0, :, rows, :] = ref[LAYERS, :, rows, :]
    ref[LAYERS + 1, :, rows, :] = ref[1, :, rows, :]


def kernel(
    where_ref,
    labels_ref,
    dens_ref,
    near_ref,
    far_ref,
    grains_ref,
    out_ref,
    lab,
    c0,
    c1,
    cx,
    mu,
    k1,
    s2,
    k2,
    lab_copies,
    c_copies,
    w_copies,
    eta_mid,
    eta_edge,
):
    grain = where_ref[0]
    core = lax.rem(grain, 2)
    start = 2 * grain - TILE + LAYERS

    def place(layer):
        z = wrap(start + layer)

        def put(ref, row, value):
            for half in range(2):
                ref[layer, half, row : row + 8, :] = value[:, half * HALF : (half + 1) * HALF]

        put(lab, MID, labels_ref[z].astype(jnp.float32))
        put(c0, MID, dens_ref[z])
        for which, ref in ((0, lab), (1, c0)):
            for block in (0, 1):
                mine = near_ref[which, block, z]
                other = far_ref[which, block, z]
                put(ref, MID + 8 * (block + 1), jnp.where(core == 0, mine, other))
                put(ref, MID - 8 * (block + 1), jnp.where(core == 0, other, mine))

    chunks(0, DEEP, place, 17)

    grain_ids = [(grain * GDEV + g).astype(jnp.float32) for g in range(GDEV)]

    def own_grains(labels, weights):
        result = []
        for g in range(GDEV):
            total = None
            for one, weight in zip(labels, weights):
                total = plus(total, jnp.where(one == grain_ids[g], weight, 0.0))
            result.append(rate * total)
        return result

    def first_sums(layer, row):
        cs = stencil(c0, layer, row)
        labs = stencil(lab, layer, row)
        for half in range(2):
            labels = [one[half] for one in labs]
            weights = [one[half] for one in cs]
            weights[0] = centre_weight(weights[0])
            square, cube = class_sums(labels, weights)
            square = (rate * rate) * square
            k1[layer, half, row : row + 8, :] = (4.0 * rate**3) * cube - 6.0 * square
            if abs(row - MID) < 16:
                s2[layer, half, row : row + 8, :] = square
            if row == MID:
                for g, value in enumerate(own_grains(labels, weights)):
                    eta_mid[layer, half, 8 * g : 8 * g + 8, :] = value

    def sums_all(layer):
        for row in (MID - 8, MID, MID + 8):
            first_sums(layer, row)

    def sums_far(layer):
        for row in (MID - 16, MID + 16):
            first_sums(layer, row)

    chunks(1, LAYERS + 1, sums_all, 2)
    close_ends(eta_mid, slice(0, 8 * GDEV))
    chunks(TILE - 6, TILE + 8, sums_far, 2)

    sub = lax.broadcasted_iota(jnp.int32, (8, HALF), 0)
    upper = sub < 4

    def edge_stencil(ref, layer):
        def both(z, offset):
            high = halves_of(ref, z, MID + 8 + offset)
            low = halves_of(ref, z, MID - 8 + offset)
            return tuple(jnp.where(upper, h, w) for h, w in zip(high, low))

        here = both(layer, 0)
        return (
            here,
            both(layer + 1, 0),
            both(layer - 1, 0),
            both(layer, 1),
            both(layer, -1),
            along(here, 1),
            along(here, -1),
        )

    def edge_grains(layer):
        cs = edge_stencil(c0, layer)
        labs = edge_stencil(lab, layer)
        for half in range(2):
            weights = [one[half] for one in cs]
            weights[0] = centre_weight(weights[0])
            for g, value in enumerate(own_grains([one[half] for one in labs], weights)):
                eta_edge[layer, half, 8 * g : 8 * g + 8, :] = value

    chunks(1, LAYERS + 1, edge_grains, 4)

    def mu_at(source, extra, layer, row):
        cs = stencil(source, layer, row)
        for half in range(2):
            c = cs[0][half]
            bulk = c * (24.0 + c * (32.0 * c - 48.0)) + extra[layer, half, row : row + 8, :]
            mu[layer, half, row : row + 8, :] = bulk - six([one[half] for one in cs[1:]])

    def c_at(source, layer, row):
        ms = stencil(mu, layer, row)
        result = []
        for half in range(2):
            c = source[layer, half, row : row + 8, :]
            lap = six([one[half] for one in ms[1:]]) - 6.0 * ms[0][half]
            result.append(c + density_step * lap)
        return result

    def over(low, high, rows, body):
        if high > low and rows:

            def step(layer):
                for row in rows:
                    body(layer, row)

            chunks(low, high, step, GROUP if len(rows) > 1 else 2 * GROUP)

    sides = (MID - 8, MID + 8)
    fars = (MID - 16, MID + 16)

    def near_tile(distance):
        return TILE - distance, TILE + 2 + distance

    def passes(extra, source, target):
        def put_mu(layer, row):
            mu_at(source, extra, layer, row)

        def put_c(layer, row):
            for half, value in enumerate(c_at(source, layer, row)):
                target[layer, half, row : row + 8, :] = value

        return put_mu, put_c

    near_rows = slice(MID - 8, MID + 16)
    for sub_step in range(1, NSUB + 1):
        source = c0 if sub_step == 1 else (cx, c1)[sub_step % 2]
        target = (c1, cx)[sub_step % 2]
        put_mu, put_c = passes(k1, source, target)
        over(1, LAYERS + 1, (MID,) + sides, put_mu)
        close_ends(mu, near_rows)
        if 8 - 2 * sub_step >= 0:
            over(*near_tile(8 - 2 * sub_step), fars, put_mu)
        if sub_step < NSUB:
            over(1, LAYERS + 1, (MID,) + sides, put_c)
            close_ends(target, near_rows)
            if 7 - 2 * sub_step >= 0:
                over(*near_tile(7 - 2 * sub_step), fars, put_c)
        else:
            over(1, LAYERS + 1, (MID,), put_c)
            over(*near_tile(7), sides, put_c)

    def grain_steps(layer):
        cs = halves_of(c1, layer, MID)
        squares = halves_of(s2, layer, MID)
        linear = [
            1.0 - rate * (12.0 * (1.0 - c) + 12.0 * square + 6.0) for c, square in zip(cs, squares)
        ]
        quadratic = [(12.0 * rate) * (2.0 - c) for c in cs]
        z = wrap(start + layer)
        for g in range(GDEV):
            mid = halves_of(eta_mid, layer, 8 * g)
            edge = halves_of(eta_edge, layer, 8 * g)
            up = halves_of(eta_mid, layer + 1, 8 * g)
            down = halves_of(eta_mid, layer - 1, 8 * g)
            right = along(mid, 1)
            left = along(mid, -1)
            for half in range(2):
                here = mid[half]
                after = rolled(jnp.where(sub == 0, edge[half], here), 1, 0)
                before = rolled(jnp.where(sub == 7, edge[half], here), -1, 0)
                around = six((up[half], down[half], after, before, right[half], left[half]))
                grains_ref[g, z, :, half * HALF : (half + 1) * HALF] = (
                    here * (linear[half] + quadratic[half] * here) + rate * around
                )

    chunks(1, LAYERS + 1, grain_steps, 8)

    def copies(index):
        layer = index + BASE
        for base, count in ((MID - 16, 16), (MID, 16), (MID + 16, 8)):
            c_here = halves_of(c0, layer, base, count)
            lab_here = halves_of(lab, layer, base, count)
            for dy in range(-2, 3):
                c_cols = along(c_here, dy) if dy else c_here
                lab_cols = along(lab_here, dy) if dy else lab_here
                rows = slice(base - MID + 16, base - MID + 16 + count)
                for half in range(2):
                    c_copies[dy + 2, index, half, rows, :] = c_cols[half]
                    lab_copies[dy + 2, index, half, rows, :] = lab_cols[half]
                    if abs(dy) < 2:
                        w_copies[dy + 1, index, half, rows, :] = centre_weight(c_cols[half])

    chunks(0, 20, copies, 5)

    def second_sums(load, c, square):
        labels = [load(lab_copies, 2, cell) for cell in INNER + OUTER]
        weights = [load(w_copies, 1, cell) for cell in INNER]
        first = [weights[0]] + [load(c_copies, 2, cell) for cell in INNER[1:]]
        spread = [6.0 * load(c_copies, 2, INNER[0])] + weights[1:]
        for cell in OUTER:
            value = load(c_copies, 2, cell)
            if 2 not in cell and -2 not in cell:
                value = value + value
            spread.append(value)
        linear = rate - (rate * rate) * (12.0 * (1.0 - c) + 12.0 * square + 6.0)
        quadratic = (12.0 * rate**3) * (2.0 - c)
        inner = None
        outer = None
        for i in range(25):
            rest = None
            own_rest = None
            for j in range(i + 1, 25):
                same = labels[i] == labels[j]
                rest = plus(rest, jnp.where(same, spread[j], 0.0))
                if j < 7:
                    own_rest = plus(own_rest, jnp.where(same, first[j], 0.0))
            total = spread[i] if rest is None else rest + spread[i]
            if i < 7:
                own = first[i] if own_rest is None else own_rest + first[i]
                value = own * (linear + quadratic * own) + (rate * rate) * total
                inner = plus(inner, value * value * (4.0 * value - 6.0))
                value = (rate * rate) * rest
                if own_rest is not None:
                    value = own_rest * (linear + quadratic * own_rest) + value
                inner = inner - value * value * (4.0 * value - 6.0)
            else:
                both = total if rest is None else total + rest
                part = both * ((4.0 * rate * rate) * both - 6.0)
                if rest is not None:
                    part = part - (4.0 * rate * rate) * (total * rest)
                outer = plus(outer, spread[i] * part)
        return inner + (rate**4) * outer

    def load_block(layer, block, half):
        def load(ref, middle, cell):
            dz, dx, dy = cell
            row = 8 + 8 * block + dx
            return ref[dy + middle, layer - BASE + dz, half, row : row + 8, :]

        return load

    def halves(low, high, body):
        def step(index, carry):
            body(lax.div(index, 2), lax.rem(index, 2))
            return carry

        lax.fori_loop(2 * low, 2 * high, step, 0)

    def plain(block):
        row = MID - 8 + 8 * block

        def body(layer, half):
            k2[layer, half, row : row + 8, :] = second_sums(
                load_block(layer, block, half),
                c1[layer, half, row : row + 8, :],
                s2[layer, half, row : row + 8, :],
            )

        return body

    def merged(layer, half):
        high = load_block(layer, 2, half)
        low = load_block(layer, 0, half)

        def load(ref, middle, cell):
            return jnp.where(upper, high(ref, middle, cell), low(ref, middle, cell))

        def field(ref):
            return jnp.where(
                upper, ref[layer, half, MID + 8 : MID + 16, :], ref[layer, half, MID - 8 : MID, :]
            )

        value = second_sums(load, field(c1), field(s2))
        k2[layer, half, MID + 8 : MID + 16, :] = value
        k2[layer, half, MID - 8 : MID, :] = value

    halves(TILE - 7, TILE + 9, plain(1))
    halves(TILE - 2, TILE + 4, plain(0))
    halves(TILE - 2, TILE + 4, plain(2))
    halves(TILE - 6, TILE - 2, merged)
    halves(TILE + 4, TILE + 8, merged)

    for sub_step in range(1, NSUB + 1):
        source = (cx, c1)[sub_step % 2]
        target = (c1, cx)[sub_step % 2]
        put_mu, put_c = passes(k2, source, target)
        over(*near_tile(9 - 2 * sub_step), (MID,), put_mu)
        over(*near_tile(8 - 2 * sub_step), sides, put_mu)
        if sub_step < NSUB:
            over(*near_tile(8 - 2 * sub_step), (MID,), put_c)
            over(*near_tile(7 - 2 * sub_step), sides, put_c)
        else:
            for layer in (0, 1):
                for half, value in enumerate(c_at(source, TILE + layer, MID)):
                    out_ref[layer, :, half * HALF : (half + 1) * HALF] = value


def sintering(where, labels, dens, near, far):
    field = pltpu.VMEM((DEEP, 2, ROWS, HALF), jnp.float32)
    vmem = pl.BlockSpec(memory_space=pltpu.VMEM)
    return pl.pallas_call(
        kernel,
        out_shape=(
            jax.ShapeDtypeStruct((GDEV, LAYERS, 8, WIDTH), jnp.float32),
            jax.ShapeDtypeStruct((2, 8, WIDTH), jnp.float32),
        ),
        in_specs=[pl.BlockSpec(memory_space=pltpu.SMEM)] + [vmem] * 4,
        out_specs=(vmem, vmem),
        scratch_shapes=[field] * 8
        + [
            pltpu.VMEM((5, 20, 2, 40, HALF), jnp.float32),
            pltpu.VMEM((5, 20, 2, 40, HALF), jnp.float32),
            pltpu.VMEM((3, 20, 2, 40, HALF), jnp.float32),
            pltpu.VMEM((DEEP, 2, 8 * GDEV, HALF), jnp.float32),
            pltpu.VMEM((DEEP, 2, 8 * GDEV, HALF), jnp.float32),
        ],
        compiler_params=pltpu.CompilerParams(vmem_limit_bytes=56 * 1024 * 1024),
        name="sintering",
    )(where, labels, dens, near, far)


def from_sides(block, distance):
    grains = lax.axis_size("grain")
    count = lax.axis_size("space")
    pairs = []
    for g in range(grains):
        way = distance if g % 2 == 0 else -distance
        for s in range(count):
            pairs.append((g * count + (s + way) % count, g * count + s))
    return lax.ppermute(block, ("grain", "space"), pairs)


def swap_cores(block):
    return lax.ppermute(block, "grain", [(i, i ^ 1) for i in range(lax.axis_size("grain"))])


def per_device(labels, density):
    grain = lax.axis_index("grain")
    named = labels.astype(jnp.float32)
    own = jnp.broadcast_to(density[None], (lax.axis_size("grain"),) + density.shape)
    dens = lax.all_to_all(own, "grain", 0, 0).reshape(LAYERS, 8, WIDTH)
    named_sides = [from_sides(named, distance) for distance in (1, 2)]
    dens_sides = [from_sides(dens, distance) for distance in (1, 2)]
    near = jnp.stack([jnp.stack(named_sides), jnp.stack(dens_sides)])
    far = swap_cores(near)
    return sintering(grain.reshape(1).astype(jnp.int32), labels, dens, near, far)


def solution(mesh):
    return jax.shard_map(
        per_device,
        mesh=mesh,
        in_specs=(P(None, "space", None), P("grain", "space", None)),
        out_specs=(P("grain", None, "space", None), P("grain", "space", None)),
        check_vma=False,
    )
```

time: 92 us -> 77.2 us (0.84)
  Pallas kernels: 45.4 us -> 30.6 us
    pallas_call x1, Pallas kernels: 45.4 us -> 30.6 us  [sintering(): pl.pallas_call(kernel, out_shape=(jax.ShapeDtypeStruct((GDEV, LAYERS, 8,...]
where the time goes in v3:
time: 77.2 us; the launch traced here: 76.8 us
  Pallas kernels  30.6 us (40%)
  starting transfers between devices  23.7 us (31%)
  waiting for transfers between devices  19.1 us (25%)
  local copies, waits for them, and re-layouts  2.47 us (3%)
    pallas_call x1, Pallas kernels, sintering(): pl.pallas_call(kernel, out_shape=(jax.ShapeDtypeStruct((GDEV, LAYERS, 8,...  30.6 us
    ppermute x4, waiting for transfers between devices, from_sides(): return lax.ppermute(block, ('grain', 'space'), pairs)  12 us
    all_to_all x1, starting transfers between devices, per_device(): dens = lax.all_to_all(own, 'grain', 0, 0).reshape(LAYERS, 8, WIDTH)  10.3 us
    ppermute x4, starting transfers between devices, from_sides(): return lax.ppermute(block, ('grain', 'space'), pairs)  8.12 us
    ppermute x1, starting transfers between devices, swap_cores(): lax.ppermute(block, 'grain', [(i, i ^ 1) for i in range(lax.axis_size('gr...  5.3 us
    all_to_all x1, waiting for transfers between devices, per_device(): dens = lax.all_to_all(own, 'grain', 0, 0).reshape(LAYERS, 8, WIDTH)  4.83 us
    ppermute x1, waiting for transfers between devices, swap_cores(): lax.ppermute(block, 'grain', [(i, i ^ 1) for i in range(lax.axis_size('gr...  2.26 us
  transfers between devices with their start and end apart: 6, of which 6 were waited for; matrix products, arithmetic and copies ran while one was open for 0% of the time, Pallas kernels for 0%

profile of v3, /device:TPU:1, one launch (start us, length us, event | category | flops | bytes accessed | tf_op | source)
XLA Modules:
  0.0 76.8 jit_solution(7943339729468389349)
XLA Ops:
  0.6 1.4 %broadcast_in_dim.2 = f32[16,2,8,256]{3,2,1,0:T(8,128)} broadcast(f32[2,8,256]{2,1,0:T(8,128)} %param.3), dimensions={1,2,3} | broadcast | bytes 278528 | tf_op jit(solution)/shard_map/broadcast_in_dim | solution.py:483
  2.1 0.0 copy-start.2
  2.1 10.3 %all-to-all-start = ((f32[16,2,8,256]{3,2,1,0:T(8,128)}), f32[16,2,8,256]{3,2,1,0:T(8,128)S(1)}, u32[]{:S(2)}, u32[]{:S(2)}) async-start(f32[16,2,8,256]{3,2,1,0:T(8,128)} %broadcast_in_dim.2), calls=%async_computation | async-start | bytes 524288 | tf_op jit(solution)/shard_map/all_to_all | solution.py:484
  12.4 0.0 copy-done.2
  12.4 1.9 %collective-permute-start.1 = (f32[32,8,256]{2,1,0:T(8,128)S(1)}, f32[32,8,256]{2,1,0:T(8,128)S(1)}, u32[]{:S(2)}, u32[]{:S(2)}) collective-permute-start(f32[32,8,256]{2,1,0:T(8,128)S(1)} %convert_element_type.3), channel_id=1, source_target_pairs={{2,0},{3,1},{4,2},{5,3},{6,4},{7,5},{8,6},{9,7},{10,8},{11,9},{12,... | collective-permute-start | bytes 786440 | tf_op jit(solution)/shard_map/ppermute | solution.py:473
  14.4 2.2 %collective-permute-start = (f32[32,8,256]{2,1,0:T(8,128)S(1)}, f32[32,8,256]{2,1,0:T(8,128)S(1)}, u32[]{:S(2)}, u32[]{:S(2)}) collective-permute-start(f32[32,8,256]{2,1,0:T(8,128)S(1)} %convert_element_type.3), channel_id=1, source_target_pairs={{1,0},{2,1},{3,2},{4,3},{5,4},{6,5},{7,6},{8,7},{9,8},{10,9},{11,1... | collective-permute-start | bytes 786440 | tf_op jit(solution)/shard_map/ppermute | solution.py:473
  16.6 4.8 %all-to-all-done = f32[16,2,8,256]{3,2,1,0:T(8,128)S(1)} async-done(((f32[16,2,8,256]{3,2,1,0:T(8,128)}), f32[16,2,8,256]{3,2,1,0:T(8,128)S(1)}, u32[]{:S(2)}, u32[]{:S(2)}) %all-to-all-start) | async-done | bytes 262176 | tf_op jit(solution)/shard_map/all_to_all | solution.py:484
  21.4 0.0 copy-start.3
  21.4 1.9 %collective-permute-start.3 = (f32[32,8,256]{2,1,0:T(8,128)S(1)}, f32[32,8,256]{2,1,0:T(8,128)S(1)}, u32[]{:S(2)}, u32[]{:S(2)}) collective-permute-start(f32[32,8,256]{2,1,0:T(8,128)S(1)} %bitcast.10), channel_id=1, source_target_pairs={{2,0},{3,1},{4,2},{5,3},{6,4},{7,5},{8,6},{9,7},{10,8},{11,9},{12,... | collective-permute-start | bytes 786440 | tf_op jit(solution)/shard_map/ppermute | solution.py:473
  23.3 2.1 %collective-permute-start.2 = (f32[32,8,256]{2,1,0:T(8,128)S(1)}, f32[32,8,256]{2,1,0:T(8,128)S(1)}, u32[]{:S(2)}, u32[]{:S(2)}) collective-permute-start(f32[32,8,256]{2,1,0:T(8,128)S(1)} %bitcast.11), channel_id=1, source_target_pairs={{1,0},{2,1},{3,2},{4,3},{5,4},{6,5},{7,6},{8,7},{9,8},{10,9},{11,1... | collective-permute-start | bytes 786440 | tf_op jit(solution)/shard_map/ppermute | solution.py:473
  25.4 0.1 collective-permute-done.1
  25.6 3.0 %collective-permute-done = f32[32,8,256]{2,1,0:T(8,128)S(1)} collective-permute-done((f32[32,8,256]{2,1,0:T(8,128)S(1)}, f32[32,8,256]{2,1,0:T(8,128)S(1)}, u32[]{:S(2)}, u32[]{:S(2)}) %collective-permute-start) | collective-permute-done | bytes 262176 | tf_op jit(solution)/shard_map/ppermute | solution.py:473
  28.6 0.0 copy-done.3
  28.6 5.9 %collective-permute-done.3 = f32[32,8,256]{2,1,0:T(8,128)S(1)} collective-permute-done((f32[32,8,256]{2,1,0:T(8,128)S(1)}, f32[32,8,256]{2,1,0:T(8,128)S(1)}, u32[]{:S(2)}, u32[]{:S(2)}) %collective-permute-start.3) | collective-permute-done | bytes 262176 | tf_op jit(solution)/shard_map/ppermute | solution.py:473
  34.5 2.9 %collective-permute-done.2 = f32[32,8,256]{2,1,0:T(8,128)S(1)} collective-permute-done((f32[32,8,256]{2,1,0:T(8,128)S(1)}, f32[32,8,256]{2,1,0:T(8,128)S(1)}, u32[]{:S(2)}, u32[]{:S(2)}) %collective-permute-start.2) | collective-permute-done | bytes 262176 | tf_op jit(solution)/shard_map/ppermute | solution.py:473
  37.5 0.1 pad_maximum_fusion.near_ref
  37.6 0.0 copy-start
  37.6 5.3 %collective-permute-start.4 = (f32[2,2,32,8,256]{4,3,2,1,0:T(8,128)S(1)}, f32[2,2,32,8,256]{4,3,2,1,0:T(8,128)S(1)}, u32[]{:S(2)}, u32[]{:S(2)}) collective-permute-start(f32[2,2,32,8,256]{4,3,2,1,0:T(8,128)S(1)} %pad_maximum_fusion.near_ref), channel_id=1, source_target_pairs={{0,32},{32,0},{64,96},{96,64},{128,160},{160,128},{192,224},{224,1... | collective-permute-start | bytes 3145736 | tf_op jit(solution)/shard_map/ppermute | solution.py:477
  42.9 2.3 %collective-permute-done.4.far_ref = f32[2,2,32,8,256]{4,3,2,1,0:T(8,128)S(1)} collective-permute-done((f32[2,2,32,8,256]{4,3,2,1,0:T(8,128)S(1)}, f32[2,2,32,8,256]{4,3,2,1,0:T(8,128)S(1)}, u32[]{:S(2)}, u32[]{:S(2)}) %collective-permute-start.4) | collective-permute-done | bytes 1048608 | tf_op jit(solution)/shard_map/ppermute | solution.py:477
  45.2 0.0 copy-start.1
  45.2 0.0 copy-done
  45.2 1.0 %copy-done.1 = f32[2,2,32,8,256]{4,3,2,1,0:T(8,128)} copy-done((f32[2,2,32,8,256]{4,3,2,1,0:T(8,128)}, f32[2,2,32,8,256]{4,3,2,1,0:T(8,128)S(1)}, u32[]{:S(2)}) %copy-start.1) | copy-done | bytes 1048600
  46.2 30.6 %sintering.1 = (f32[4,32,8,256]{3,2,1,0:T(8,128)}, f32[2,8,256]{2,1,0:T(8,128)}) custom-call(s32[1]{0:T(128)} %bitcast.where_ref, s32[32,8,256]{2,1,0:T(8,128)} %labels_ref.1, f32[32,8,256]{2,1,0:T(8,128)} %bitcast.12, f32[2,2,32,8,256]{4,3,2,1,0:T(8,128)} %copy-done, f32[2,2,32,8,256]{4,3,2,1,0:T(8,128)} %copy-done.1), custom_call_target="tpu_custom_call" | custom-call | tf_op jit(solution)/shard_map/sintering/pallas_call | solution.py:444
  (3 shorter events, 0.1 us)
Async XLA Ops:
  2.1 10.3 %copy-start.2 = (s32[32,8,256]{2,1,0:T(8,128)S(1)}, s32[32,8,256]{2,1,0:T(8,128)}, u32[]{:S(2)}) copy-start(s32[32,8,256]{2,1,0:T(8,128)} %labels_ref.1) | copy-start | bytes 786436
  2.1 19.3 %all-to-all-start = ((f32[16,2,8,256]{3,2,1,0:T(8,128)}), f32[16,2,8,256]{3,2,1,0:T(8,128)S(1)}, u32[]{:S(2)}, u32[]{:S(2)}) async-start(f32[16,2,8,256]{3,2,1,0:T(8,128)} %broadcast_in_dim.2), calls=%async_computation | async-start | bytes 524288 | tf_op jit(solution)/shard_map/all_to_all | solution.py:484
  12.4 13.1 %collective-permute-start.1 = (f32[32,8,256]{2,1,0:T(8,128)S(1)}, f32[32,8,256]{2,1,0:T(8,128)S(1)}, u32[]{:S(2)}, u32[]{:S(2)}) collective-permute-start(f32[32,8,256]{2,1,0:T(8,128)S(1)} %convert_element_type.3), channel_id=1, source_target_pairs={{2,0},{3,1},{4,2},{5,3},{6,4},{7,5},{8,6},{9,7},{10,8},{11,9},{12,... | collective-permute-start | bytes 786440 | tf_op jit(solution)/shard_map/ppermute | solution.py:473
  14.4 14.2 %collective-permute-start = (f32[32,8,256]{2,1,0:T(8,128)S(1)}, f32[32,8,256]{2,1,0:T(8,128)S(1)}, u32[]{:S(2)}, u32[]{:S(2)}) collective-permute-start(f32[32,8,256]{2,1,0:T(8,128)S(1)} %convert_element_type.3), channel_id=1, source_target_pairs={{1,0},{2,1},{3,2},{4,3},{5,4},{6,5},{7,6},{8,7},{9,8},{10,9},{11,1... | collective-permute-start | bytes 786440 | tf_op jit(solution)/shard_map/ppermute | solution.py:473
  21.4 7.2 %copy-start.3 = (f32[16,2,8,256]{3,2,1,0:T(8,128)}, f32[16,2,8,256]{3,2,1,0:T(8,128)S(1)}, u32[]{:S(2)}) copy-start(f32[16,2,8,256]{3,2,1,0:T(8,128)S(1)} %all-to-all-done) | copy-start | bytes 786436
  21.4 13.1 %collective-permute-start.3 = (f32[32,8,256]{2,1,0:T(8,128)S(1)}, f32[32,8,256]{2,1,0:T(8,128)S(1)}, u32[]{:S(2)}, u32[]{:S(2)}) collective-permute-start(f32[32,8,256]{2,1,0:T(8,128)S(1)} %bitcast.10), channel_id=1, source_target_pairs={{2,0},{3,1},{4,2},{5,3},{6,4},{7,5},{8,6},{9,7},{10,8},{11,9},{12,... | collective-permute-start | bytes 786440 | tf_op jit(solution)/shard_map/ppermute | solution.py:473
  23.3 14.2 %collective-permute-start.2 = (f32[32,8,256]{2,1,0:T(8,128)S(1)}, f32[32,8,256]{2,1,0:T(8,128)S(1)}, u32[]{:S(2)}, u32[]{:S(2)}) collective-permute-start(f32[32,8,256]{2,1,0:T(8,128)S(1)} %bitcast.11), channel_id=1, source_target_pairs={{1,0},{2,1},{3,2},{4,3},{5,4},{6,5},{7,6},{8,7},{9,8},{10,9},{11,1... | collective-permute-start | bytes 786440 | tf_op jit(solution)/shard_map/ppermute | solution.py:473
  37.6 7.6 %copy-start = (f32[2,2,32,8,256]{4,3,2,1,0:T(8,128)}, f32[2,2,32,8,256]{4,3,2,1,0:T(8,128)S(1)}, u32[]{:S(2)}) copy-start(f32[2,2,32,8,256]{4,3,2,1,0:T(8,128)S(1)} %pad_maximum_fusion.near_ref) | copy-start | bytes 3145732
  37.6 7.6 %collective-permute-start.4 = (f32[2,2,32,8,256]{4,3,2,1,0:T(8,128)S(1)}, f32[2,2,32,8,256]{4,3,2,1,0:T(8,128)S(1)}, u32[]{:S(2)}, u32[]{:S(2)}) collective-permute-start(f32[2,2,32,8,256]{4,3,2,1,0:T(8,128)S(1)} %pad_maximum_fusion.near_ref), channel_id=1, source_target_pairs={{0,32},{32,0},{64,96},{96,64},{128,160},{160,128},{192,224},{224,1... | collective-permute-start | bytes 3145736 | tf_op jit(solution)/shard_map/ppermute | solution.py:477
  45.2 1.0 %copy-start.1 = (f32[2,2,32,8,256]{4,3,2,1,0:T(8,128)}, f32[2,2,32,8,256]{4,3,2,1,0:T(8,128)S(1)}, u32[]{:S(2)}) copy-start(f32[2,2,32,8,256]{4,3,2,1,0:T(8,128)S(1)} %collective-permute-done.4.far_ref) | copy-start | bytes 3145732

commit v4 on v3

--- a/solution.py
+++ b/solution.py
@@ -123,9 +123,11 @@
     where_ref,
     labels_ref,
     dens_ref,
-    near_ref,
-    far_ref,
-    grains_ref,
+    near_labels_ref,
+    near_dens_ref,
+    far_labels_ref,
+    far_dens_ref,
+    grains_out,
     out_ref,
     lab,
     c0,
@@ -140,28 +142,41 @@
     w_copies,
     eta_mid,
     eta_edge,
+    grains_ref,
+    far_dens,
+    sems,
 ):
     grain = where_ref[0]
     core = lax.rem(grain, 2)
     start = 2 * grain - TILE + LAYERS
 
+    incoming = pltpu.make_async_copy(far_dens_ref, far_dens, sems.at[0])
+    incoming.start()
+    near_rows = [MID + 8 * (block + 1) * (1 - 2 * core) for block in (0, 1)]
+    far_rows = [MID - 8 * (block + 1) * (1 - 2 * core) for block in (0, 1)]
+
+    def put(ref, layer, row, value):
+        for half in range(2):
+            part = value[:, half * HALF : (half + 1) * HALF]
+            ref[layer, half, pl.ds(pl.multiple_of(row, 8), 8), :] = part
+
     def place(layer):
         z = wrap(start + layer)
-
-        def put(ref, row, value):
-            for half in range(2):
-                ref[layer, half, row : row + 8, :] = value[:, half * HALF : (half + 1) * HALF]
-
-        put(lab, MID, labels_ref[z].astype(jnp.float32))
-        put(c0, MID, dens_ref[z])
-        for which, ref in ((0, lab), (1, c0)):
-            for block in (0, 1):
-                mine = near_ref[which, block, z]
-                other = far_ref[which, block, z]
-                put(ref, MID + 8 * (block + 1), jnp.where(core == 0, mine, other))
-                put(ref, MID - 8 * (block + 1), jnp.where(core == 0, other, mine))
+        put(lab, layer, MID, labels_ref[z].astype(jnp.float32))
+        put(c0, layer, MID, dens_ref[z])
+        for block in (0, 1):
+            put(lab, layer, near_rows[block], near_labels_ref[block, z])
+            put(lab, layer, far_rows[block], far_labels_ref[block, z])
+            put(c0, layer, near_rows[block], near_dens_ref[block, z])
+
+    def place_far(layer):
+        z = wrap(start + layer)
+        for block in (0, 1):
+            put(c0, layer, far_rows[block], far_dens[block, z])
 
     chunks(0, DEEP, place, 17)
+    incoming.wait()
+    chunks(0, DEEP, place_far, 17)
 
     grain_ids = [(grain * GDEV + g).astype(jnp.float32) for g in range(GDEV)]
 
@@ -274,18 +289,18 @@
 
         return put_mu, put_c
 
-    near_rows = slice(MID - 8, MID + 16)
+    span = slice(MID - 8, MID + 16)
     for sub_step in range(1, NSUB + 1):
         source = c0 if sub_step == 1 else (cx, c1)[sub_step % 2]
         target = (c1, cx)[sub_step % 2]
         put_mu, put_c = passes(k1, source, target)
         over(1, LAYERS + 1, (MID,) + sides, put_mu)
-        close_ends(mu, near_rows)
+        close_ends(mu, span)
         if 8 - 2 * sub_step >= 0:
             over(*near_tile(8 - 2 * sub_step), fars, put_mu)
         if sub_step < NSUB:
             over(1, LAYERS + 1, (MID,) + sides, put_c)
-            close_ends(target, near_rows)
+            close_ends(target, span)
             if 7 - 2 * sub_step >= 0:
                 over(*near_tile(7 - 2 * sub_step), fars, put_c)
         else:
@@ -317,6 +332,8 @@
                 )
 
     chunks(1, LAYERS + 1, grain_steps, 8)
+    outgoing = pltpu.make_async_copy(grains_ref, grains_out, sems.at[1])
+    outgoing.start()
 
     def copies(index):
         layer = index + BASE
@@ -436,19 +453,21 @@
             for layer in (0, 1):
                 for half, value in enumerate(c_at(source, TILE + layer, MID)):
                     out_ref[layer, :, half * HALF : (half + 1) * HALF] = value
-
-
-def sintering(where, labels, dens, near, far):
+    outgoing.wait()
+
+
+def sintering(where, labels, dens, near_labels, near_dens, far_labels, far_dens):
     field = pltpu.VMEM((DEEP, 2, ROWS, HALF), jnp.float32)
     vmem = pl.BlockSpec(memory_space=pltpu.VMEM)
+    anywhere = pl.BlockSpec(memory_space=pl.ANY)
     return pl.pallas_call(
         kernel,
         out_shape=(
             jax.ShapeDtypeStruct((GDEV, LAYERS, 8, WIDTH), jnp.float32),
             jax.ShapeDtypeStruct((2, 8, WIDTH), jnp.float32),
         ),
-        in_specs=[pl.BlockSpec(memory_space=pltpu.SMEM)] + [vmem] * 4,
-        out_specs=(vmem, vmem),
+        in_specs=[pl.BlockSpec(memory_space=pltpu.SMEM)] + [vmem] * 5 + [anywhere],
+        out_specs=(anywhere, vmem),
         scratch_shapes=[field] * 8
         + [
             pltpu.VMEM((5, 20, 2, 40, HALF), jnp.float32),
@@ -456,10 +475,13 @@
             pltpu.VMEM((3, 20, 2, 40, HALF), jnp.float32),
             pltpu.VMEM((DEEP, 2, 8 * GDEV, HALF), jnp.float32),
             pltpu.VMEM((DEEP, 2, 8 * GDEV, HALF), jnp.float32),
+            pltpu.VMEM((GDEV, LAYERS, 8, WIDTH), jnp.float32),
+            pltpu.VMEM((2, LAYERS, 8, WIDTH), jnp.float32),
+            pltpu.SemaphoreType.DMA((2,)),
         ],
         compiler_params=pltpu.CompilerParams(vmem_limit_bytes=56 * 1024 * 1024),
         name="sintering",
-    )(where, labels, dens, near, far)
+    )(where, labels, dens, near_labels, near_dens, far_labels, far_dens)
 
 
 def from_sides(block, distance):
@@ -482,11 +504,21 @@
     named = labels.astype(jnp.float32)
     own = jnp.broadcast_to(density[None], (lax.axis_size("grain"),) + density.shape)
     dens = lax.all_to_all(own, "grain", 0, 0).reshape(LAYERS, 8, WIDTH)
-    named_sides = [from_sides(named, distance) for distance in (1, 2)]
-    dens_sides = [from_sides(dens, distance) for distance in (1, 2)]
-    near = jnp.stack([jnp.stack(named_sides), jnp.stack(dens_sides)])
-    far = swap_cores(near)
-    return sintering(grain.reshape(1).astype(jnp.int32), labels, dens, near, far)
+    far_side, near_side = [from_sides(named, distance) for distance in (2, 1)]
+    near_labels = jnp.stack([near_side, far_side])
+    far_side, near_side = [from_sides(dens, distance) for distance in (2, 1)]
+    near_dens = jnp.stack([near_side, far_side])
+    far_labels = swap_cores(near_labels)
+    far_dens = swap_cores(near_dens)
+    return sintering(
+        grain.reshape(1).astype(jnp.int32),
+        labels,
+        dens,
+        near_labels,
+        near_dens,
+        far_labels,
+        far_dens,
+    )
 
 
 def solution(mesh):

time: 77.2 us -> 76.7 us (level)
  waiting for transfers between devices: 19.1 us -> 10.5 us
  starting transfers between devices: 23.7 us -> 31.5 us
    ppermute x4, waiting for transfers between devices: 12 us -> 4.22 us  [from_sides(): return lax.ppermute(block, ('grain', 'space'), pairs)]
    ppermute x1 -> x2, starting transfers between devices: 5.3 us -> 13 us  [swap_cores(): lax.ppermute(block, 'grain', [(i, i ^ 1) for i in range(lax.axis_size('gr...]
    ppermute x1 -> x2, waiting for transfers between devices: 2.26 us -> 1.49 us  [swap_cores(): lax.ppermute(block, 'grain', [(i, i ^ 1) for i in range(lax.axis_size('gr...]
  transfers between devices with their start and end apart: 6 -> 7, of which waited for: 6 -> 5; matrix products, arithmetic and copies ran while one was open for 0% -> 0% of each run, Pallas kernels for 0% -> 0%
where the time goes in v4:
time: 76.7 us; the launch traced here: 76.2 us
  starting transfers between devices  31.5 us (41%)
  Pallas kernels  31 us (40%)
  waiting for transfers between devices  10.5 us (14%)
  local copies, waits for them, and re-layouts  2.26 us (3%)
    pallas_call x1, Pallas kernels, sintering(): pl.pallas_call(kernel, out_shape=(jax.ShapeDtypeStruct((GDEV, LAYERS, 8,...  31 us
    ppermute x2, starting transfers between devices, swap_cores(): lax.ppermute(block, 'grain', [(i, i ^ 1) for i in range(lax.axis_size('gr...  13 us
    all_to_all x1, starting transfers between devices, per_device(): dens = lax.all_to_all(own, 'grain', 0, 0).reshape(LAYERS, 8, WIDTH)  10.3 us
    ppermute x4, starting transfers between devices, from_sides(): return lax.ppermute(block, ('grain', 'space'), pairs)  8.12 us
    all_to_all x1, waiting for transfers between devices, per_device(): dens = lax.all_to_all(own, 'grain', 0, 0).reshape(LAYERS, 8, WIDTH)  4.83 us
    ppermute x4, waiting for transfers between devices, from_sides(): return lax.ppermute(block, ('grain', 'space'), pairs)  4.22 us
  transfers between devices with their start and end apart: 7, of which 5 were waited for; matrix products, arithmetic and copies ran while one was open for 0% of the time, Pallas kernels for 0%

profile of v4, /device:TPU:1, one launch (start us, length us, event | category | flops | bytes accessed | tf_op | source)
XLA Modules:
  0.0 76.2 jit_solution(12758955826549440936)
XLA Ops:
  0.6 1.4 %broadcast_in_dim.2 = f32[16,2,8,256]{3,2,1,0:T(8,128)} broadcast(f32[2,8,256]{2,1,0:T(8,128)} %param.3), dimensions={1,2,3} | broadcast | bytes 278528 | tf_op jit(solution)/shard_map/broadcast_in_dim | solution.py:505
  2.1 0.0 copy-start.2
  2.1 10.3 %all-to-all-start = ((f32[16,2,8,256]{3,2,1,0:T(8,128)}), f32[16,2,8,256]{3,2,1,0:T(8,128)S(1)}, u32[]{:S(2)}, u32[]{:S(2)}) async-start(f32[16,2,8,256]{3,2,1,0:T(8,128)} %broadcast_in_dim.2), calls=%async_computation | async-start | bytes 524288 | tf_op jit(solution)/shard_map/all_to_all | solution.py:506
  12.4 0.0 copy-done.2
  12.4 1.9 %collective-permute-start.1 = (f32[32,8,256]{2,1,0:T(8,128)S(1)}, f32[32,8,256]{2,1,0:T(8,128)S(1)}, u32[]{:S(2)}, u32[]{:S(2)}) collective-permute-start(f32[32,8,256]{2,1,0:T(8,128)S(1)} %convert_element_type.3), channel_id=1, source_target_pairs={{2,0},{3,1},{4,2},{5,3},{6,4},{7,5},{8,6},{9,7},{10,8},{11,9},{12,... | collective-permute-start | bytes 786440 | tf_op jit(solution)/shard_map/ppermute | solution.py:495
  14.4 2.2 %collective-permute-start = (f32[32,8,256]{2,1,0:T(8,128)S(1)}, f32[32,8,256]{2,1,0:T(8,128)S(1)}, u32[]{:S(2)}, u32[]{:S(2)}) collective-permute-start(f32[32,8,256]{2,1,0:T(8,128)S(1)} %convert_element_type.3), channel_id=1, source_target_pairs={{1,0},{2,1},{3,2},{4,3},{5,4},{6,5},{7,6},{8,7},{9,8},{10,9},{11,1... | collective-permute-start | bytes 786440 | tf_op jit(solution)/shard_map/ppermute | solution.py:495
  16.6 4.8 %all-to-all-done = f32[16,2,8,256]{3,2,1,0:T(8,128)S(1)} async-done(((f32[16,2,8,256]{3,2,1,0:T(8,128)}), f32[16,2,8,256]{3,2,1,0:T(8,128)S(1)}, u32[]{:S(2)}, u32[]{:S(2)}) %all-to-all-start) | async-done | bytes 262176 | tf_op jit(solution)/shard_map/all_to_all | solution.py:506
  21.4 0.0 copy-start.3
  21.4 1.9 %collective-permute-start.3 = (f32[32,8,256]{2,1,0:T(8,128)S(1)}, f32[32,8,256]{2,1,0:T(8,128)S(1)}, u32[]{:S(2)}, u32[]{:S(2)}) collective-permute-start(f32[32,8,256]{2,1,0:T(8,128)S(1)} %bitcast.6), channel_id=1, source_target_pairs={{2,0},{3,1},{4,2},{5,3},{6,4},{7,5},{8,6},{9,7},{10,8},{11,9},{12,... | collective-permute-start | bytes 786440 | tf_op jit(solution)/shard_map/ppermute | solution.py:495
  23.3 2.1 %collective-permute-start.2 = (f32[32,8,256]{2,1,0:T(8,128)S(1)}, f32[32,8,256]{2,1,0:T(8,128)S(1)}, u32[]{:S(2)}, u32[]{:S(2)}) collective-permute-start(f32[32,8,256]{2,1,0:T(8,128)S(1)} %bitcast.7), channel_id=1, source_target_pairs={{1,0},{2,1},{3,2},{4,3},{5,4},{6,5},{7,6},{8,7},{9,8},{10,9},{11,1... | collective-permute-start | bytes 786440 | tf_op jit(solution)/shard_map/ppermute | solution.py:495
  25.4 0.1 collective-permute-done.1
  25.6 3.0 %collective-permute-done = f32[32,8,256]{2,1,0:T(8,128)S(1)} collective-permute-done((f32[32,8,256]{2,1,0:T(8,128)S(1)}, f32[32,8,256]{2,1,0:T(8,128)S(1)}, u32[]{:S(2)}, u32[]{:S(2)}) %collective-permute-start) | collective-permute-done | bytes 262176 | tf_op jit(solution)/shard_map/ppermute | solution.py:495
  28.6 0.0 copy-done.3
  28.6 0.0 copy-start
  28.7 7.7 %collective-permute-start.4 = (f32[2,32,8,256]{3,2,1,0:T(8,128)S(1)}, f32[2,32,8,256]{3,2,1,0:T(8,128)S(1)}, u32[]{:S(2)}, u32[]{:S(2)}) collective-permute-start(f32[2,32,8,256]{3,2,1,0:T(8,128)S(1)} %pad_maximum_fusion.near_labels_ref), channel_id=1, source_target_pairs={{0,32},{32,0},{64,96},{96,64},{128,160},{160,128},{192,224},{224,1... | collective-permute-start | bytes 1572872 | tf_op jit(solution)/shard_map/ppermute | solution.py:499
  36.4 0.0 collective-permute-done.3
  36.4 1.0 %collective-permute-done.2 = f32[32,8,256]{2,1,0:T(8,128)S(1)} collective-permute-done((f32[32,8,256]{2,1,0:T(8,128)S(1)}, f32[32,8,256]{2,1,0:T(8,128)S(1)}, u32[]{:S(2)}, u32[]{:S(2)}) %collective-permute-start.2) | collective-permute-done | bytes 262176 | tf_op jit(solution)/shard_map/ppermute | solution.py:495
  37.5 0.0 copy-done
  37.5 0.0 copy-start.1
  37.5 5.3 %collective-permute-start.5 = (f32[2,32,8,256]{3,2,1,0:T(8,128)S(1)}, f32[2,32,8,256]{3,2,1,0:T(8,128)S(1)}, u32[]{:S(2)}, u32[]{:S(2)}) collective-permute-start(f32[2,32,8,256]{3,2,1,0:T(8,128)S(1)} %pad_maximum_fusion.1.near_dens_ref), channel_id=1, source_target_pairs={{0,32},{32,0},{64,96},{96,64},{128,160},{160,128},{192,224},{224,1... | collective-permute-start | bytes 1572872 | tf_op jit(solution)/shard_map/ppermute | solution.py:499
  42.8 0.0 collective-permute-done.4.far_labels_ref
  42.8 0.0 copy-start.4
  42.9 1.5 %collective-permute-done.5.far_dens_ref = f32[2,32,8,256]{3,2,1,0:T(8,128)S(1)} collective-permute-done((f32[2,32,8,256]{3,2,1,0:T(8,128)S(1)}, f32[2,32,8,256]{3,2,1,0:T(8,128)S(1)}, u32[]{:S(2)}, u32[]{:S(2)}) %collective-permute-start.5) | collective-permute-done | bytes 524320 | tf_op jit(solution)/shard_map/ppermute | solution.py:499
  44.3 0.0 copy-start.5
  44.3 0.0 copy-done.1
  44.3 0.0 copy-done.4
  44.3 0.8 %copy-done.5 = f32[2,32,8,256]{3,2,1,0:T(8,128)} copy-done((f32[2,32,8,256]{3,2,1,0:T(8,128)}, f32[2,32,8,256]{3,2,1,0:T(8,128)S(1)}, u32[]{:S(2)}) %copy-start.5) | copy-done | bytes 524312
  45.1 31.0 %sintering.1 = (f32[4,32,8,256]{3,2,1,0:T(8,128)}, f32[2,8,256]{2,1,0:T(8,128)}) custom-call(s32[1]{0:T(128)} %bitcast.where_ref, s32[32,8,256]{2,1,0:T(8,128)} %labels_ref.1, f32[32,8,256]{2,1,0:T(8,128)} %bitcast.8, f32[2,32,8,256]{3,2,1,0:T(8,128)} %copy-done, f32[2,32,8,256]{3,2,1,0:T(8,128)} %copy-done.1, f32[2,32,8,256]{3,2,1,0:T(8,128)} %copy-done.4, ...), custom_call_target="tpu_custom_call" | custom-call | tf_op jit(solution)/shard_map/sintering/pallas_call | solution.py:463
  (3 shorter events, 0.1 us)
Async XLA Ops:
  2.1 10.3 %copy-start.2 = (s32[32,8,256]{2,1,0:T(8,128)S(1)}, s32[32,8,256]{2,1,0:T(8,128)}, u32[]{:S(2)}) copy-start(s32[32,8,256]{2,1,0:T(8,128)} %labels_ref.1) | copy-start | bytes 786436
  2.1 19.3 %all-to-all-start = ((f32[16,2,8,256]{3,2,1,0:T(8,128)}), f32[16,2,8,256]{3,2,1,0:T(8,128)S(1)}, u32[]{:S(2)}, u32[]{:S(2)}) async-start(f32[16,2,8,256]{3,2,1,0:T(8,128)} %broadcast_in_dim.2), calls=%async_computation | async-start | bytes 524288 | tf_op jit(solution)/shard_map/all_to_all | solution.py:506
  12.4 13.1 %collective-permute-start.1 = (f32[32,8,256]{2,1,0:T(8,128)S(1)}, f32[32,8,256]{2,1,0:T(8,128)S(1)}, u32[]{:S(2)}, u32[]{:S(2)}) collective-permute-start(f32[32,8,256]{2,1,0:T(8,128)S(1)} %convert_element_type.3), channel_id=1, source_target_pairs={{2,0},{3,1},{4,2},{5,3},{6,4},{7,5},{8,6},{9,7},{10,8},{11,9},{12,... | collective-permute-start | bytes 786440 | tf_op jit(solution)/shard_map/ppermute | solution.py:495
  14.4 14.2 %collective-permute-start = (f32[32,8,256]{2,1,0:T(8,128)S(1)}, f32[32,8,256]{2,1,0:T(8,128)S(1)}, u32[]{:S(2)}, u32[]{:S(2)}) collective-permute-start(f32[32,8,256]{2,1,0:T(8,128)S(1)} %convert_element_type.3), channel_id=1, source_target_pairs={{1,0},{2,1},{3,2},{4,3},{5,4},{6,5},{7,6},{8,7},{9,8},{10,9},{11,1... | collective-permute-start | bytes 786440 | tf_op jit(solution)/shard_map/ppermute | solution.py:495
  21.4 7.2 %copy-start.3 = (f32[16,2,8,256]{3,2,1,0:T(8,128)}, f32[16,2,8,256]{3,2,1,0:T(8,128)S(1)}, u32[]{:S(2)}) copy-start(f32[16,2,8,256]{3,2,1,0:T(8,128)S(1)} %all-to-all-done) | copy-start | bytes 786436
  21.4 15.0 %collective-permute-start.3 = (f32[32,8,256]{2,1,0:T(8,128)S(1)}, f32[32,8,256]{2,1,0:T(8,128)S(1)}, u32[]{:S(2)}, u32[]{:S(2)}) collective-permute-start(f32[32,8,256]{2,1,0:T(8,128)S(1)} %bitcast.6), channel_id=1, source_target_pairs={{2,0},{3,1},{4,2},{5,3},{6,4},{7,5},{8,6},{9,7},{10,8},{11,9},{12,... | collective-permute-start | bytes 786440 | tf_op jit(solution)/shard_map/ppermute | solution.py:495
  23.3 14.2 %collective-permute-start.2 = (f32[32,8,256]{2,1,0:T(8,128)S(1)}, f32[32,8,256]{2,1,0:T(8,128)S(1)}, u32[]{:S(2)}, u32[]{:S(2)}) collective-permute-start(f32[32,8,256]{2,1,0:T(8,128)S(1)} %bitcast.7), channel_id=1, source_target_pairs={{1,0},{2,1},{3,2},{4,3},{5,4},{6,5},{7,6},{8,7},{9,8},{10,9},{11,1... | collective-permute-start | bytes 786440 | tf_op jit(solution)/shard_map/ppermute | solution.py:495
  28.6 8.9 %copy-start = (f32[2,32,8,256]{3,2,1,0:T(8,128)}, f32[2,32,8,256]{3,2,1,0:T(8,128)S(1)}, u32[]{:S(2)}) copy-start(f32[2,32,8,256]{3,2,1,0:T(8,128)S(1)} %pad_maximum_fusion.near_labels_ref) | copy-start | bytes 1572868
  28.7 14.2 %collective-permute-start.4 = (f32[2,32,8,256]{3,2,1,0:T(8,128)S(1)}, f32[2,32,8,256]{3,2,1,0:T(8,128)S(1)}, u32[]{:S(2)}, u32[]{:S(2)}) collective-permute-start(f32[2,32,8,256]{3,2,1,0:T(8,128)S(1)} %pad_maximum_fusion.near_labels_ref), channel_id=1, source_target_pairs={{0,32},{32,0},{64,96},{96,64},{128,160},{160,128},{192,224},{224,1... | collective-permute-start | bytes 1572872 | tf_op jit(solution)/shard_map/ppermute | solution.py:499
  37.5 6.8 %copy-start.1 = (f32[2,32,8,256]{3,2,1,0:T(8,128)}, f32[2,32,8,256]{3,2,1,0:T(8,128)S(1)}, u32[]{:S(2)}) copy-start(f32[2,32,8,256]{3,2,1,0:T(8,128)S(1)} %pad_maximum_fusion.1.near_dens_ref) | copy-start | bytes 1572868
  37.5 6.8 %collective-permute-start.5 = (f32[2,32,8,256]{3,2,1,0:T(8,128)S(1)}, f32[2,32,8,256]{3,2,1,0:T(8,128)S(1)}, u32[]{:S(2)}, u32[]{:S(2)}) collective-permute-start(f32[2,32,8,256]{3,2,1,0:T(8,128)S(1)} %pad_maximum_fusion.1.near_dens_ref), channel_id=1, source_target_pairs={{0,32},{32,0},{64,96},{96,64},{128,160},{160,128},{192,224},{224,1... | collective-permute-start | bytes 1572872 | tf_op jit(solution)/shard_map/ppermute | solution.py:499
  42.8 1.5 %copy-start.4 = (f32[2,32,8,256]{3,2,1,0:T(8,128)}, f32[2,32,8,256]{3,2,1,0:T(8,128)S(1)}, u32[]{:S(2)}) copy-start(f32[2,32,8,256]{3,2,1,0:T(8,128)S(1)} %collective-permute-done.4.far_labels_ref) | copy-start | bytes 1572868
  44.3 0.8 %copy-start.5 = (f32[2,32,8,256]{3,2,1,0:T(8,128)}, f32[2,32,8,256]{3,2,1,0:T(8,128)S(1)}, u32[]{:S(2)}) copy-start(f32[2,32,8,256]{3,2,1,0:T(8,128)S(1)} %collective-permute-done.5.far_dens_ref) | copy-start | bytes 1572868

commit v5 on v4

--- a/solution.py
+++ b/solution.py
@@ -144,6 +144,7 @@
     eta_edge,
     grains_ref,
     far_dens,
+    triples,
     sems,
 ):
     grain = where_ref[0]
@@ -352,43 +353,143 @@
 
     chunks(0, 20, copies, 5)
 
-    def second_sums(load, c, square):
-        labels = [load(lab_copies, 2, cell) for cell in INNER + OUTER]
-        weights = [load(w_copies, 1, cell) for cell in INNER]
-        first = [weights[0]] + [load(c_copies, 2, cell) for cell in INNER[1:]]
-        spread = [6.0 * load(c_copies, 2, INNER[0])] + weights[1:]
+    odd = lax.rem(sub, 2) == 1
+    lane = lax.broadcasted_iota(jnp.int32, (8, HALF), 1)
+    early = lax.rem(lane, 8) < 4
+
+    def swapped(value, step):
+        bit = lax.rem(lax.div(lane, step), 2) == 1
+        return jnp.where(bit, rolled(value, -step, 1), rolled(value, step, 1))
+
+    def block_labels(pair):
+        for block in range(3):
+            row = MID - 8 + 8 * block
+            for half in range(2):
+                cells = []
+                for layer in (2 * pair, 2 * pair + 1):
+                    cells.append(lab[layer, half, row : row + 8, :])
+                    after = lab[layer, half, row + 1 : row + 9, :]
+                    before = lab[layer, half, row - 1 : row + 7, :]
+                    cells.append(jnp.where(odd, before, after))
+
+                def over_block(pick, values):
+                    result = pick(pick(values[0], values[1]), pick(values[2], values[3]))
+                    for step in (1, 2, 4):
+                        result = pick(result, swapped(result, step))
+                    return result
+
+                high = over_block(jnp.maximum, cells)
+                low = over_block(jnp.minimum, cells)
+                others = [
+                    jnp.where(cell == high, -1.0, jnp.where(cell == low, -1.0, cell))
+                    for cell in cells
+                ]
+                middle = over_block(jnp.maximum, others)
+                low = jnp.where(low == high, -1.0, low)
+                for slot, value in enumerate((high, middle, low)):
+                    triples[slot, pair - 4, half, 8 * block : 8 * block + 8, :] = value
+
+    chunks(4, 13, block_labels, 3)
+
+    def second_sums(load, own_labels, c, square, out):
+        labels = {cell: load(lab_copies, 2, cell) for cell in INNER + OUTER}
+        spread = {cell: load(w_copies, 1, cell) for cell in INNER}
+        first = {cell: load(c_copies, 2, cell) for cell in INNER}
+        spread[INNER[0]], first[INNER[0]] = 6.0 * first[INNER[0]], spread[INNER[0]]
         for cell in OUTER:
             value = load(c_copies, 2, cell)
-            if 2 not in cell and -2 not in cell:
-                value = value + value
-            spread.append(value)
+            spread[cell] = value if 2 in cell or -2 in cell else value + value
         linear = rate - (rate * rate) * (12.0 * (1.0 - c) + 12.0 * square + 6.0)
         quadratic = (12.0 * rate**3) * (2.0 - c)
+
+        def settled(own, total):
+            value = (rate * rate) * total
+            if own is not None:
+                value = own * (linear + quadratic * own) + value
+            return value * value * (4.0 * value - 6.0)
+
+        taken = {}
+        taken_first = {}
         inner = None
+        for one in own_labels:
+            total = None
+            own = None
+            for cell in INNER + OUTER:
+                same = labels[cell] == one
+                part = jnp.where(same, spread[cell], 0.0)
+                total = plus(total, part)
+                taken[cell] = plus(taken.get(cell), part)
+                if cell in first:
+                    part = jnp.where(same, first[cell], 0.0)
+                    own = plus(own, part)
+                    taken_first[cell] = plus(taken_first.get(cell), part)
+            inner = plus(inner, settled(own, total))
+        left = {cell: spread[cell] - taken[cell] for cell in INNER[1:] + OUTER}
+        left_first = {cell: first[cell] - taken_first[cell] for cell in INNER[1:]}
+
+        def by(mask, one, two):
+            return (
+                jnp.where(mask, labels[one], labels[two]),
+                left[one] + left[two],
+                left_first[one] + left_first[two] if one in left_first else None,
+            )
+
+        def alone(cell):
+            return labels[cell], left[cell], left_first.get(cell)
+
+        slots = [
+            alone((out, 0, 0)),
+            by(odd, (0, 1, 0), (0, -1, 0)),
+            by(early, (0, 0, -1), (0, 0, 1)),
+            alone((2, 0, 0)),
+            alone((-2, 0, 0)),
+            alone((out, 0, 1)),
+            alone((out, 0, -1)),
+            alone((out, 1, 0)),
+            alone((out, -1, 0)),
+            by(odd, (-out, 1, 0), (-out, -1, 0)),
+            by(early, (-out, 0, -1), (-out, 0, 1)),
+            alone((0, 2, 0)),
+            alone((0, -2, 0)),
+            by(early, (0, 0, -2), (0, 0, 2)),
+        ]
+        turned = {}
+        for dy in (-1, 1):
+            one, two = (0, 1, dy), (0, -1, dy)
+            slots.append(
+                (
+                    jnp.where(odd, labels[one], labels[two]),
+                    jnp.where(odd, left[one], left[two]),
+                    None,
+                )
+            )
+            turned[dy] = (
+                jnp.where(odd, labels[two], labels[one]),
+                jnp.where(odd, left[two], left[one]),
+            )
+        slots.append(
+            (jnp.where(early, turned[-1][0], turned[1][0]), turned[-1][1] + turned[1][1], None)
+        )
+
         outer = None
-        for i in range(25):
+        for i, (label, weight, weight_first) in enumerate(slots):
             rest = None
             own_rest = None
-            for j in range(i + 1, 25):
-                same = labels[i] == labels[j]
-                rest = plus(rest, jnp.where(same, spread[j], 0.0))
-                if j < 7:
-                    own_rest = plus(own_rest, jnp.where(same, first[j], 0.0))
-            total = spread[i] if rest is None else rest + spread[i]
-            if i < 7:
-                own = first[i] if own_rest is None else own_rest + first[i]
-                value = own * (linear + quadratic * own) + (rate * rate) * total
-                inner = plus(inner, value * value * (4.0 * value - 6.0))
-                value = (rate * rate) * rest
-                if own_rest is not None:
-                    value = own_rest * (linear + quadratic * own_rest) + value
-                inner = inner - value * value * (4.0 * value - 6.0)
+            for other, value, value_first in slots[i + 1 :]:
+                same = label == other
+                rest = plus(rest, jnp.where(same, value, 0.0))
+                if value_first is not None:
+                    own_rest = plus(own_rest, jnp.where(same, value_first, 0.0))
+            if weight_first is not None:
+                own = weight_first if own_rest is None else own_rest + weight_first
+                inner = inner + settled(own, rest + weight) - settled(own_rest, rest)
             else:
+                total = weight if rest is None else rest + weight
                 both = total if rest is None else total + rest
                 part = both * ((4.0 * rate * rate) * both - 6.0)
                 if rest is not None:
                     part = part - (4.0 * rate * rate) * (total * rest)
-                outer = plus(outer, spread[i] * part)
+                outer = plus(outer, weight * part)
         return inner + (rate**4) * outer
 
     def load_block(layer, block, half):
@@ -399,26 +500,34 @@
 
         return load
 
+    def own_block(layer, block, half):
+        pair = lax.div(layer, 2) - 4
+        return [triples[slot, pair, half, 8 * block : 8 * block + 8, :] for slot in range(3)]
+
     def halves(low, high, body):
         def step(index, carry):
-            body(lax.div(index, 2), lax.rem(index, 2))
+            layer = low + 2 * lax.div(index, 2)
+            for k in range(2):
+                body(layer + k, lax.rem(index, 2), 1 if (low + k) % 2 else -1)
             return carry
 
-        lax.fori_loop(2 * low, 2 * high, step, 0)
+        lax.fori_loop(0, high - low, step, 0)
 
     def plain(block):
         row = MID - 8 + 8 * block
 
-        def body(layer, half):
+        def body(layer, half, out):
             k2[layer, half, row : row + 8, :] = second_sums(
                 load_block(layer, block, half),
+                own_block(layer, block, half),
                 c1[layer, half, row : row + 8, :],
                 s2[layer, half, row : row + 8, :],
+                out,
             )
 
         return body
 
-    def merged(layer, half):
+    def merged(layer, half, out):
         high = load_block(layer, 2, half)
         low = load_block(layer, 0, half)
 
@@ -430,7 +539,11 @@
                 upper, ref[layer, half, MID + 8 : MID + 16, :], ref[layer, half, MID - 8 : MID, :]
             )
 
-        value = second_sums(load, field(c1), field(s2))
+        own_labels = [
+            jnp.where(upper, one, two)
+            for one, two in zip(own_block(layer, 2, half), own_block(layer, 0, half))
+        ]
+        value = second_sums(load, own_labels, field(c1), field(s2), out)
         k2[layer, half, MID + 8 : MID + 16, :] = value
         k2[layer, half, MID - 8 : MID, :] = value
 
@@ -477,9 +590,10 @@
             pltpu.VMEM((DEEP, 2, 8 * GDEV, HALF), jnp.float32),
             pltpu.VMEM((GDEV, LAYERS, 8, WIDTH), jnp.float32),
             pltpu.VMEM((2, LAYERS, 8, WIDTH), jnp.float32),
+            pltpu.VMEM((3, 9, 2, 24, HALF), jnp.float32),
             pltpu.SemaphoreType.DMA((2,)),
         ],
-        compiler_params=pltpu.CompilerParams(vmem_limit_bytes=56 * 1024 * 1024),
+        compiler_params=pltpu.CompilerParams(vmem_limit_bytes=38 * 1024 * 1024),
         name="sintering",
     )(where, labels, dens, near_labels, near_dens, far_labels, far_dens)
 

time: 76.7 us -> 72 us (0.939)
  Pallas kernels: 31 us -> 27.2 us
  local copies, waits for them, and re-layouts: 2.26 us -> 1.45 us
    pallas_call x1, Pallas kernels: 31 us -> 27.2 us  [sintering(): pl.pallas_call(kernel, out_shape=(jax.ShapeDtypeStruct((GDEV, LAYERS, 8,...]
    unnamed x12 -> x2, local copies, waits for them, and re-layouts: 0.82 us -> 0.01 us
where the time goes in v5:
time: 72 us; the launch traced here: 71.6 us
  starting transfers between devices  31.5 us (44%)
  Pallas kernels  27.2 us (38%)
  waiting for transfers between devices  10.6 us (15%)
  local copies, waits for them, and re-layouts  1.45 us (2%)
  between operations  0.72 us (1%)
    pallas_call x1, Pallas kernels, sintering(): pl.pallas_call(kernel, out_shape=(jax.ShapeDtypeStruct((GDEV, LAYERS, 8,...  27.2 us
    ppermute x2, starting transfers between devices, swap_cores(): lax.ppermute(block, 'grain', [(i, i ^ 1) for i in range(lax.axis_size('gr...  13 us
    all_to_all x1, starting transfers between devices, per_device(): dens = lax.all_to_all(own, 'grain', 0, 0).reshape(LAYERS, 8, WIDTH)  10.3 us
    ppermute x4, starting transfers between devices, from_sides(): return lax.ppermute(block, ('grain', 'space'), pairs)  8.12 us
    all_to_all x1, waiting for transfers between devices, per_device(): dens = lax.all_to_all(own, 'grain', 0, 0).reshape(LAYERS, 8, WIDTH)  4.83 us
    ppermute x4, waiting for transfers between devices, from_sides(): return lax.ppermute(block, ('grain', 'space'), pairs)  4.24 us
    ppermute x2, waiting for transfers between devices, swap_cores(): lax.ppermute(block, 'grain', [(i, i ^ 1) for i in range(lax.axis_size('gr...  1.5 us
    broadcast_in_dim x1, local copies, waits for them, and re-layouts, per_device(): jnp.broadcast_to(density[None], (lax.axis_size('grain'),) + density.shape)  1.45 us
  transfers between devices with their start and end apart: 7, of which 5 were waited for; matrix products, arithmetic and copies ran while one was open for 0% of the time, Pallas kernels for 0%

profile of v5, /device:TPU:1, one launch (start us, length us, event | category | flops | bytes accessed | tf_op | source)
XLA Modules:
  0.0 71.6 jit_solution(16662116913815931709)
XLA Ops:
  0.6 1.4 %broadcast_in_dim.2 = f32[16,2,8,256]{3,2,1,0:T(8,128)} broadcast(f32[2,8,256]{2,1,0:T(8,128)} %param.3), dimensions={1,2,3} | broadcast | bytes 278528 | tf_op jit(solution)/shard_map/broadcast_in_dim | solution.py:619
  2.1 0.0 copy-start
  2.1 10.3 %all-to-all-start = ((f32[16,2,8,256]{3,2,1,0:T(8,128)}), f32[16,2,8,256]{3,2,1,0:T(8,128)S(1)}, u32[]{:S(2)}, u32[]{:S(2)}) async-start(f32[16,2,8,256]{3,2,1,0:T(8,128)} %broadcast_in_dim.2), calls=%async_computation | async-start | bytes 524288 | tf_op jit(solution)/shard_map/all_to_all | solution.py:620
  12.4 0.0 copy-done
  12.4 1.9 %collective-permute-start.1 = (f32[32,8,256]{2,1,0:T(8,128)S(1)}, f32[32,8,256]{2,1,0:T(8,128)S(1)}, u32[]{:S(2)}, u32[]{:S(2)}) collective-permute-start(f32[32,8,256]{2,1,0:T(8,128)S(1)} %convert_element_type.3), channel_id=1, source_target_pairs={{2,0},{3,1},{4,2},{5,3},{6,4},{7,5},{8,6},{9,7},{10,8},{11,9},{12,... | collective-permute-start | bytes 786440 | tf_op jit(solution)/shard_map/ppermute | solution.py:609
  14.4 2.2 %collective-permute-start = (f32[32,8,256]{2,1,0:T(8,128)S(1)}, f32[32,8,256]{2,1,0:T(8,128)S(1)}, u32[]{:S(2)}, u32[]{:S(2)}) collective-permute-start(f32[32,8,256]{2,1,0:T(8,128)S(1)} %convert_element_type.3), channel_id=1, source_target_pairs={{1,0},{2,1},{3,2},{4,3},{5,4},{6,5},{7,6},{8,7},{9,8},{10,9},{11,1... | collective-permute-start | bytes 786440 | tf_op jit(solution)/shard_map/ppermute | solution.py:609
  16.6 4.8 %all-to-all-done = f32[16,2,8,256]{3,2,1,0:T(8,128)S(1)} async-done(((f32[16,2,8,256]{3,2,1,0:T(8,128)}), f32[16,2,8,256]{3,2,1,0:T(8,128)S(1)}, u32[]{:S(2)}, u32[]{:S(2)}) %all-to-all-start) | async-done | bytes 262176 | tf_op jit(solution)/shard_map/all_to_all | solution.py:620
  21.4 1.9 %collective-permute-start.3 = (f32[32,8,256]{2,1,0:T(8,128)S(1)}, f32[32,8,256]{2,1,0:T(8,128)S(1)}, u32[]{:S(2)}, u32[]{:S(2)}) collective-permute-start(f32[32,8,256]{2,1,0:T(8,128)S(1)} %bitcast.6), channel_id=1, source_target_pairs={{2,0},{3,1},{4,2},{5,3},{6,4},{7,5},{8,6},{9,7},{10,8},{11,9},{12,... | collective-permute-start | bytes 786440 | tf_op jit(solution)/shard_map/ppermute | solution.py:609
  23.3 2.1 %collective-permute-start.2 = (f32[32,8,256]{2,1,0:T(8,128)S(1)}, f32[32,8,256]{2,1,0:T(8,128)S(1)}, u32[]{:S(2)}, u32[]{:S(2)}) collective-permute-start(f32[32,8,256]{2,1,0:T(8,128)S(1)} %bitcast.7), channel_id=1, source_target_pairs={{1,0},{2,1},{3,2},{4,3},{5,4},{6,5},{7,6},{8,7},{9,8},{10,9},{11,1... | collective-permute-start | bytes 786440 | tf_op jit(solution)/shard_map/ppermute | solution.py:609
  25.4 0.1 collective-permute-done.1
  25.6 3.0 %collective-permute-done = f32[32,8,256]{2,1,0:T(8,128)S(1)} collective-permute-done((f32[32,8,256]{2,1,0:T(8,128)S(1)}, f32[32,8,256]{2,1,0:T(8,128)S(1)}, u32[]{:S(2)}, u32[]{:S(2)}) %collective-permute-start) | collective-permute-done | bytes 262176 | tf_op jit(solution)/shard_map/ppermute | solution.py:609
  28.6 7.7 %collective-permute-start.4 = (f32[2,32,8,256]{3,2,1,0:T(8,128)S(1)}, f32[2,32,8,256]{3,2,1,0:T(8,128)S(1)}, u32[]{:S(2)}, u32[]{:S(2)}) collective-permute-start(f32[2,32,8,256]{3,2,1,0:T(8,128)S(1)} %pad_maximum_fusion.near_labels_ref), channel_id=1, source_target_pairs={{0,32},{32,0},{64,96},{96,64},{128,160},{160,128},{192,224},{224,1... | collective-permute-start | bytes 1572872 | tf_op jit(solution)/shard_map/ppermute | solution.py:613
  36.4 0.0 collective-permute-done.3
  36.4 1.1 %collective-permute-done.2 = f32[32,8,256]{2,1,0:T(8,128)S(1)} collective-permute-done((f32[32,8,256]{2,1,0:T(8,128)S(1)}, f32[32,8,256]{2,1,0:T(8,128)S(1)}, u32[]{:S(2)}, u32[]{:S(2)}) %collective-permute-start.2) | collective-permute-done | bytes 262176 | tf_op jit(solution)/shard_map/ppermute | solution.py:609
  37.5 5.3 %collective-permute-start.5 = (f32[2,32,8,256]{3,2,1,0:T(8,128)S(1)}, f32[2,32,8,256]{3,2,1,0:T(8,128)S(1)}, u32[]{:S(2)}, u32[]{:S(2)}) collective-permute-start(f32[2,32,8,256]{3,2,1,0:T(8,128)S(1)} %pad_maximum_fusion.1.near_dens_ref), channel_id=1, source_target_pairs={{0,32},{32,0},{64,96},{96,64},{128,160},{160,128},{192,224},{224,1... | collective-permute-start | bytes 1572872 | tf_op jit(solution)/shard_map/ppermute | solution.py:613
  42.8 0.0 collective-permute-done.4.far_labels_ref
  42.8 1.5 %collective-permute-done.5.far_dens_ref = f32[2,32,8,256]{3,2,1,0:T(8,128)S(1)} collective-permute-done((f32[2,32,8,256]{3,2,1,0:T(8,128)S(1)}, f32[2,32,8,256]{3,2,1,0:T(8,128)S(1)}, u32[]{:S(2)}, u32[]{:S(2)}) %collective-permute-start.5) | collective-permute-done | bytes 524320 | tf_op jit(solution)/shard_map/ppermute | solution.py:613
  44.3 27.2 %sintering.1 = (f32[4,32,8,256]{3,2,1,0:T(8,128)}, f32[2,8,256]{2,1,0:T(8,128)}) custom-call(s32[1]{0:T(128)} %bitcast.where_ref, s32[32,8,256]{2,1,0:T(8,128)S(1)} %copy-done, f32[32,8,256]{2,1,0:T(8,128)S(1)} %bitcast.8, f32[2,32,8,256]{3,2,1,0:T(8,128)S(1)} %pad_maximum_fusion.near_labels_ref, f32[2,32,8,256]{3,2,1,0:T(8,128)S(1)} %pad_maximum_fusion.1.near_dens_ref, ...), custom_call_target="tpu_custom_call" | custom-call | tf_op jit(solution)/shard_map/sintering/pallas_call | solution.py:576
  (3 shorter events, 0.1 us)
Async XLA Ops:
  2.1 10.3 %copy-start = (s32[32,8,256]{2,1,0:T(8,128)S(1)}, s32[32,8,256]{2,1,0:T(8,128)}, u32[]{:S(2)}) copy-start(s32[32,8,256]{2,1,0:T(8,128)} %labels_ref.1) | copy-start | bytes 786436
  2.1 19.3 %all-to-all-start = ((f32[16,2,8,256]{3,2,1,0:T(8,128)}), f32[16,2,8,256]{3,2,1,0:T(8,128)S(1)}, u32[]{:S(2)}, u32[]{:S(2)}) async-start(f32[16,2,8,256]{3,2,1,0:T(8,128)} %broadcast_in_dim.2), calls=%async_computation | async-start | bytes 524288 | tf_op jit(solution)/shard_map/all_to_all | solution.py:620
  12.4 13.1 %collective-permute-start.1 = (f32[32,8,256]{2,1,0:T(8,128)S(1)}, f32[32,8,256]{2,1,0:T(8,128)S(1)}, u32[]{:S(2)}, u32[]{:S(2)}) collective-permute-start(f32[32,8,256]{2,1,0:T(8,128)S(1)} %convert_element_type.3), channel_id=1, source_target_pairs={{2,0},{3,1},{4,2},{5,3},{6,4},{7,5},{8,6},{9,7},{10,8},{11,9},{12,... | collective-permute-start | bytes 786440 | tf_op jit(solution)/shard_map/ppermute | solution.py:609
  14.4 14.2 %collective-permute-start = (f32[32,8,256]{2,1,0:T(8,128)S(1)}, f32[32,8,256]{2,1,0:T(8,128)S(1)}, u32[]{:S(2)}, u32[]{:S(2)}) collective-permute-start(f32[32,8,256]{2,1,0:T(8,128)S(1)} %convert_element_type.3), channel_id=1, source_target_pairs={{1,0},{2,1},{3,2},{4,3},{5,4},{6,5},{7,6},{8,7},{9,8},{10,9},{11,1... | collective-permute-start | bytes 786440 | tf_op jit(solution)/shard_map/ppermute | solution.py:609
  21.4 15.0 %collective-permute-start.3 = (f32[32,8,256]{2,1,0:T(8,128)S(1)}, f32[32,8,256]{2,1,0:T(8,128)S(1)}, u32[]{:S(2)}, u32[]{:S(2)}) collective-permute-start(f32[32,8,256]{2,1,0:T(8,128)S(1)} %bitcast.6), channel_id=1, source_target_pairs={{2,0},{3,1},{4,2},{5,3},{6,4},{7,5},{8,6},{9,7},{10,8},{11,9},{12,... | collective-permute-start | bytes 786440 | tf_op jit(solution)/shard_map/ppermute | solution.py:609
  23.3 14.2 %collective-permute-start.2 = (f32[32,8,256]{2,1,0:T(8,128)S(1)}, f32[32,8,256]{2,1,0:T(8,128)S(1)}, u32[]{:S(2)}, u32[]{:S(2)}) collective-permute-start(f32[32,8,256]{2,1,0:T(8,128)S(1)} %bitcast.7), channel_id=1, source_target_pairs={{1,0},{2,1},{3,2},{4,3},{5,4},{6,5},{7,6},{8,7},{9,8},{10,9},{11,1... | collective-permute-start | bytes 786440 | tf_op jit(solution)/shard_map/ppermute | solution.py:609
  28.6 14.2 %collective-permute-start.4 = (f32[2,32,8,256]{3,2,1,0:T(8,128)S(1)}, f32[2,32,8,256]{3,2,1,0:T(8,128)S(1)}, u32[]{:S(2)}, u32[]{:S(2)}) collective-permute-start(f32[2,32,8,256]{3,2,1,0:T(8,128)S(1)} %pad_maximum_fusion.near_labels_ref), channel_id=1, source_target_pairs={{0,32},{32,0},{64,96},{96,64},{128,160},{160,128},{192,224},{224,1... | collective-permute-start | bytes 1572872 | tf_op jit(solution)/shard_map/ppermute | solution.py:613
  37.5 6.8 %collective-permute-start.5 = (f32[2,32,8,256]{3,2,1,0:T(8,128)S(1)}, f32[2,32,8,256]{3,2,1,0:T(8,128)S(1)}, u32[]{:S(2)}, u32[]{:S(2)}) collective-permute-start(f32[2,32,8,256]{3,2,1,0:T(8,128)S(1)} %pad_maximum_fusion.1.near_dens_ref), channel_id=1, source_target_pairs={{0,32},{32,0},{64,96},{96,64},{128,160},{160,128},{192,224},{224,1... | collective-permute-start | bytes 1572872 | tf_op jit(solution)/shard_map/ppermute | solution.py:613
